TPU v7x, 256 devices: a whole 4x4x8 slice. The times are simulated.
256 devices in a mesh: seq: 8 (over x, core), state: 32 (over z, y).
Axes of the slice: x: 4, y: 4, z: 8, core: 2. Of those that a mesh axis runs over, the one named last changes fastest.
Arguments:
- alpha_in: float32 [256, 131072], P('seq', 'state'), may hold values from 0.1 to 3
- beta_in: float32 [256, 131072], P('seq', 'state'), may hold values from 0.1 to 3
- transitions: bfloat16 [1024, 4, 128, 128], P('state'), may hold values from 0.049804688 to 1
- emission_cols: bfloat16 [256, 131072], P(None, 'state'), may hold values from 0.049804688 to 1
- token_ids: int32 [256, 4], P('seq'), may hold values from 0 to 255
- sources: int32 [1024, 4], replicated, may hold values from 0 to 1023, as said below
Outputs:
- counts: float32 [1024, 4, 128, 128], P('state', None, 'seq')
- alpha_end: float32 [256, 131072], P('seq', 'state')
- beta_start: float32 [256, 131072], P('seq', 'state')
- loglik: float32 [256], P('seq')
Inputs may be any that keep to these rules, and one draw needn't show every extreme that they name: `sources`: block b lies with index b // 32 of state. The 128 entries of the rows of one index of state name blocks of exactly 16 distinct indices, exactly 8 entries for each of them; which indices is drawn, and the same block may be named more than once.
All inputs are finite; a program needn't handle non-finite values.
Results may differ from a plain program's by a relative error of at most 0.0016.
Values may be sent and summed in bfloat16 or wider, within the bound.
A program may use at most 128 MiB of HBM per device.

v0:
```python
import jax
import jax.numpy as jnp
from jax import lax
from jax.sharding import PartitionSpec as P

K = 4
STEPS = 4


def shards(alpha_in, beta_in, transitions, emission_cols, token_ids, sources):
    seq_count = alpha_in.shape[0]
    local_width = alpha_in.shape[1]
    blocks = transitions.shape[0]
    block_size = transitions.shape[2]
    peer_count = lax.axis_size("state")
    rank_here = lax.axis_index("state")
    ref_count = blocks * K
    groups = peer_count // 2
    capacity = ref_count // groups
    states_total = local_width * peer_count
    own_source = lax.dynamic_slice_in_dim(sources, rank_here * blocks, blocks, 0).reshape(ref_count)
    own_owner = own_source // blocks
    ordinal = jnp.arange(ref_count, dtype=jnp.int32)
    earlier = (own_owner[None, :] == own_owner[:, None]) & (ordinal[None, :] < ordinal[:, None])
    own_slot = jnp.sum(earlier.astype(jnp.int32), axis=1)
    all_owner = sources.reshape(peer_count, ref_count) // blocks
    all_local = sources.reshape(peer_count, ref_count) % blocks
    from_here = all_owner == rank_here
    slot_all = jnp.cumsum(from_here.astype(jnp.int32), axis=1) - 1
    chosen = from_here[:, :, None] & (
        slot_all[:, :, None] == jnp.arange(capacity, dtype=jnp.int32)[None, None, :]
    )
    send_index = jnp.sum(jnp.where(chosen, all_local[:, :, None], 0), axis=1)
    filled = jnp.any(chosen, axis=1)
    collect = (
        (send_index[:, :, None] == jnp.arange(blocks, dtype=jnp.int32)[None, None, :])
        & filled[:, :, None]
    ).astype(jnp.bfloat16)
    forward = alpha_in
    loglik = jnp.zeros((seq_count,), jnp.float32)
    stored = []
    for position in range(STEPS):
        emission = jnp.take(emission_cols, token_ids[:, position], axis=0).astype(jnp.float32)
        outgoing = forward.astype(jnp.bfloat16)
        fetch_parcel = jnp.take(outgoing.reshape(seq_count, blocks, block_size), send_index, axis=1)
        arrived = lax.all_to_all(fetch_parcel, "state", split_axis=1, concat_axis=1, tiled=True)
        fetched = arrived[:, own_owner, own_slot].reshape(seq_count, blocks, K, block_size)
        mixture = jnp.einsum(
            "sjka,jkab->sjb", fetched, transitions, preferred_element_type=jnp.float32
        ).reshape(seq_count, local_width)
        scaled = emission * mixture
        factor = lax.psum(jnp.sum(scaled, axis=1), "state") / states_total
        loglik = loglik + jnp.log(factor)
        stored.append((fetched, emission, scaled))
        forward = scaled / factor[:, None]
    backward = beta_in
    counts = jnp.zeros((blocks, K, block_size, block_size), jnp.float32)
    for position in reversed(range(STEPS)):
        fetched, emission, scaled = stored[position]
        weighted = emission * backward
        pair_mean = lax.psum(jnp.sum(scaled * backward, axis=1), "state") / states_total
        posterior = (
            (weighted / pair_mean[:, None])
            .astype(jnp.bfloat16)
            .reshape(seq_count, blocks, block_size)
        )
        counts = counts + jnp.einsum(
            "sjka,sjb->jkab", fetched, posterior, preferred_element_type=jnp.float32
        )
        spread = weighted.astype(jnp.bfloat16).reshape(seq_count, blocks, block_size)
        partial_value = jnp.einsum(
            "sjb,jkab->sjka", spread, transitions, preferred_element_type=jnp.float32
        )
        partial_value = partial_value.astype(jnp.bfloat16).reshape(seq_count, ref_count, block_size)
        parcel = jnp.zeros((seq_count, peer_count, capacity, block_size), jnp.bfloat16)
        parcel = parcel.at[:, own_owner, own_slot].set(partial_value)
        returned = lax.all_to_all(parcel, "state", split_axis=1, concat_axis=1, tiled=True)
        raw_beta = jnp.einsum(
            "sxca,xcb->sba", returned, collect, preferred_element_type=jnp.float32
        ).reshape(seq_count, local_width)
        factor = lax.psum(jnp.sum(raw_beta, axis=1), "state") / states_total
        backward = raw_beta / factor[:, None]
    counts = counts * transitions.astype(jnp.float32)
    shares = lax.psum_scatter(counts, "seq", scatter_dimension=2, tiled=True)
    return (shares, forward, backward, loglik)


def solution(mesh):
    placed = (
        P("seq", "state"),
        P("seq", "state"),
        P("state", None, None, None),
        P(None, "state"),
        P("seq", None),
        P(),
    )
    return jax.shard_map(
        shards,
        mesh=mesh,
        in_specs=placed,
        out_specs=(P("state", None, "seq", None), P("seq", "state"), P("seq", "state"), P("seq")),
        check_vma=False,
    )
```

profile of v0, /device:TPU:1, one launch (start us, length us, event | category | flops | bytes accessed | tf_op | source)
XLA Modules:
  0.0 1032.2 jit_solution(14905316310905563345)
XLA Ops:
  16.4 13.7 %scatter_fusion = bf16[32,32,8,128]{3,0,2,1:T(8,128)(2,1)} fusion(bf16[32,32,8,128]{3,0,2,1:T(8,128)(2,1)} %broadcast.273.clone.2, s32[128]{0:T(128)S(1)} %get-tuple-element.26, bf16[128,32,128]{2,1,0:T(8,128)(2,1)S(1)} %bitcast.292), kind=kCustom, calls=%fused_computation.12 | custom fusion | bytes 3146752 | tf_op jit(solution)/shard_map/scatter | solution.py:76
  34.1 12.3 %all-to-all-start.4 = ((bf16[32,32,8,128]{3,2,0,1:T(8,128)(2,1)}), bf16[32,32,8,128]{3,2,0,1:T(8,128)(2,1)}, u32[]{:S(2)}, u32[]{:S(2)}) async-start(bf16[32,32,8,128]{3,2,0,1:T(8,128)(2,1)} %copy.119), calls=%async_computation.4 | async-start | bytes 4194304 | tf_op jit(solution)/shard_map/all_to_all | solution.py:77
  49.4 45.5 %all-to-all-done.4 = bf16[32,32,8,128]{3,2,0,1:T(8,128)(2,1)} async-done(((bf16[32,32,8,128]{3,2,0,1:T(8,128)(2,1)}), bf16[32,32,8,128]{3,2,0,1:T(8,128)(2,1)}, u32[]{:S(2)}, u32[]{:S(2)}) %all-to-all-start.4) | async-done | bytes 2097184 | tf_op jit(solution)/shard_map/all_to_all | solution.py:77
  97.9 57.8 %psum.88 = f32[32]{0:T(128)S(1)} all-reduce(f32[32]{0:T(128)S(1)} %get-tuple-element.43), channel_id=1, replica_groups=mesh['seq'=8,'state'=32] {'state'}, use_global_device_ids=true, to_apply=%region_14.17 | all-reduce | flops 32 | bytes 256 | tf_op jit(solution)/shard_map/psum | solution.py:81
  162.6 13.7 %scatter_fusion.1 = bf16[32,32,8,128]{3,0,2,1:T(8,128)(2,1)} fusion(bf16[32,32,8,128]{3,0,2,1:T(8,128)(2,1)} %broadcast.273.clone.1, s32[128]{0:T(128)S(1)} %get-tuple-element.26, bf16[128,32,128]{2,1,0:T(8,128)(2,1)S(1)} %bitcast.293), kind=kCustom, calls=%fused_computation.13 | custom fusion | bytes 3146752 | tf_op jit(solution)/shard_map/scatter | solution.py:76
  180.2 6.7 all-to-all-start.5
  192.0 29.9 %all-to-all-done.5 = bf16[32,32,8,128]{3,2,0,1:T(8,128)(2,1)} async-done(((bf16[32,32,8,128]{3,2,0,1:T(8,128)(2,1)}), bf16[32,32,8,128]{3,2,0,1:T(8,128)(2,1)}, u32[]{:S(2)}, u32[]{:S(2)}) %all-to-all-start.5) | async-done | bytes 2097184 | tf_op jit(solution)/shard_map/all_to_all | solution.py:77
  221.9 7.4 all-to-all-start
  233.2 83.0 %psum.90 = f32[32]{0:T(128)S(1)} all-reduce(f32[32]{0:T(128)S(1)} %get-tuple-element.45), channel_id=1, replica_groups=mesh['seq'=8,'state'=32] {'state'}, use_global_device_ids=true, to_apply=%region_19.22 | all-reduce | flops 32 | bytes 256 | tf_op jit(solution)/shard_map/psum | solution.py:81
  323.1 13.8 %scatter_fusion.2 = bf16[32,32,8,128]{3,0,2,1:T(8,128)(2,1)} fusion(bf16[32,32,8,128]{3,0,2,1:T(8,128)(2,1)} %broadcast.273.clone, s32[128]{0:T(128)S(1)} %get-tuple-element.26, bf16[128,32,128]{2,1,0:T(8,128)(2,1)S(1)} %bitcast.294), kind=kCustom, calls=%fused_computation.14 | custom fusion | bytes 3146752 | tf_op jit(solution)/shard_map/scatter | solution.py:76
  340.8 8.9 all-to-all-start.6
  356.0 21.6 %all-to-all-done.6 = bf16[32,32,8,128]{3,2,0,1:T(8,128)(2,1)} async-done(((bf16[32,32,8,128]{3,2,0,1:T(8,128)(2,1)}), bf16[32,32,8,128]{3,2,0,1:T(8,128)(2,1)}, u32[]{:S(2)}, u32[]{:S(2)}) %all-to-all-start.6) | async-done | bytes 2097184 | tf_op jit(solution)/shard_map/all_to_all | solution.py:77
  380.7 63.0 %psum.92 = f32[32]{0:T(128)S(1)} all-reduce(f32[32]{0:T(128)S(1)} %get-tuple-element.47), channel_id=1, replica_groups=mesh['seq'=8,'state'=32] {'state'}, use_global_device_ids=true, to_apply=%region_24.27 | all-reduce | flops 32 | bytes 256 | tf_op jit(solution)/shard_map/psum | solution.py:81
  444.9 55.7 %psum.84 = f32[32]{0:T(128)S(1)} all-reduce(f32[32]{0:T(128)S(1)} %get-tuple-element.9), channel_id=1, replica_groups=mesh['seq'=8,'state'=32] {'state'}, use_global_device_ids=true, to_apply=%region_4.7 | all-reduce | flops 32 | bytes 256 | tf_op jit(solution)/shard_map/psum | solution.py:52
  504.7 32.4 %all_to_all.40 = bf16[32,32,8,128]{3,0,2,1:T(8,128)(2,1)} all-to-all(bf16[32,32,8,128]{3,0,2,1:T(8,128)(2,1)S(1)} %select_bitcast_fusion.2), channel_id=1, replica_groups=mesh['seq'=8,'state'=32] {'state'}, dimensions={1} | all-to-all | bytes 4194304 | tf_op jit(solution)/shard_map/all_to_all | solution.py:46
  543.5 62.0 %psum.85 = f32[32]{0:T(128)S(1)} all-reduce(f32[32]{0:T(128)S(1)} %get-tuple-element.12), channel_id=1, replica_groups=mesh['seq'=8,'state'=32] {'state'}, use_global_device_ids=true, to_apply=%region_6.9 | all-reduce | flops 32 | bytes 256 | tf_op jit(solution)/shard_map/psum | solution.py:52
  623.6 15.5 %scatter_fusion.3 = bf16[32,32,8,128]{3,0,2,1:T(8,128)(2,1)} fusion(bf16[32,32,8,128]{3,0,2,1:T(8,128)(2,1)} %broadcast.273, s32[128]{0:T(128)S(1)} %get-tuple-element.26, bf16[128,32,128]{2,1,0:T(8,128)(2,1)} %bitcast.291), kind=kCustom, calls=%fused_computation.15 | custom fusion | bytes 3146752 | tf_op jit(solution)/shard_map/scatter | solution.py:76
  645.2 7.0 all-to-all-start.7
  660.2 73.9 %psum.86 = f32[32]{0:T(128)S(1)} all-reduce(f32[32]{0:T(128)S(1)} %get-tuple-element.11), channel_id=1, replica_groups=mesh['seq'=8,'state'=32] {'state'}, use_global_device_ids=true, to_apply=%region_8.11 | all-reduce | flops 32 | bytes 256 | tf_op jit(solution)/shard_map/psum | solution.py:52
  740.3 10.4 %all-to-all-start.3 = ((bf16[32,32,8,128]{3,0,2,1:T(8,128)(2,1)}), bf16[32,32,8,128]{3,0,2,1:T(8,128)(2,1)}, u32[]{:S(2)}, u32[]{:S(2)}) async-start(bf16[32,32,8,128]{3,0,2,1:T(8,128)(2,1)} %select_bitcast_fusion), calls=%async_computation.3 | async-start | bytes 4194304 | tf_op jit(solution)/shard_map/all_to_all | solution.py:46
  754.6 24.8 %all-to-all-done.3 = bf16[32,32,8,128]{3,0,2,1:T(8,128)(2,1)} async-done(((bf16[32,32,8,128]{3,0,2,1:T(8,128)(2,1)}), bf16[32,32,8,128]{3,0,2,1:T(8,128)(2,1)}, u32[]{:S(2)}, u32[]{:S(2)}) %all-to-all-start.3) | async-done | bytes 2097184 | tf_op jit(solution)/shard_map/all_to_all | solution.py:46
  786.9 62.3 %all-reduce = (f32[32]{0:T(128)S(1)}, f32[32]{0:T(128)S(1)}, f32[32]{0:T(128)S(1)}, f32[32]{0:T(128)S(1)}, f32[32]{0:T(128)S(1)}, /*index=5*/f32[32]{0:T(128)S(1)}) all-reduce(f32[32]{0:T(128)S(1)} %get-tuple-element.13, f32[32]{0:T(128)S(1)} %get-tuple-element.7, ...), channel_id=1, replica_groups=mesh['seq'=8,'state'=32] {'state'}, use_global_device_ids=true, to_apply=%region_21.24 | all-reduce | flops 192 | bytes 1536 | tf_op jit(solution)/shard_map/psum | solution.py:61
  867.2 13.2 %convert_multiply_fusion = f32[32,4,128,128]{3,2,1,0:T(8,128)} fusion(bf16[32,4,128,128]{3,2,1,0:T(8,128)(2,1)S(1)} %copy-done.2, f32[32,4,128,128]{3,2,1,0:T(8,128)} %fusion.19, f32[32,4,128,128]{3,2,1,0:T(8,128)} %fusion.25, f32[32,4,128,128]{3,2,1,0:T(8,128)} %fusion.22, bf16[32,32,4,128]{3,0,2,1:T(8,128)(2,1)S(1)} %bitcast.274, ...), kind=kOutput, calls=%fused_computation.16 | convolution fusion | flops 144703488 | bytes 39059456 | tf_op jit(solution)/shard_map/sjka,sjb->jkab/dot_general | solution.py:67
  882.5 142.4 %reduce-scatter.2.cloned.1.call-done = f32[32,4,16,128]{3,2,1,0:T(8,128)} async-done(((f32[32,4,128,128]{3,2,1,0:T(8,128)}), f32[32,4,16,128]{3,2,1,0:T(8,128)}) %reduce-scatter.2.cloned.1.call-update) | async-done | bytes 1048592 | tf_op jit(solution)/shard_map/reduce_scatter | solution.py:84
  (169 shorter events, 140.3 us)
Async XLA Ops:
  34.1 12.3 %copy-start.30 = (s32[1024,4]{0,1:T(4,128)S(1)}, s32[1024,4]{0,1:T(4,128)}, u32[]{:S(2)}) copy-start(s32[1024,4]{0,1:T(4,128)} %param.15) | copy-start | bytes 49156
  34.1 60.8 %all-to-all-start.4 = ((bf16[32,32,8,128]{3,2,0,1:T(8,128)(2,1)}), bf16[32,32,8,128]{3,2,0,1:T(8,128)(2,1)}, u32[]{:S(2)}, u32[]{:S(2)}) async-start(bf16[32,32,8,128]{3,2,0,1:T(8,128)(2,1)} %copy.119), calls=%async_computation.4 | async-start | bytes 4194304 | tf_op jit(solution)/shard_map/all_to_all | solution.py:77
  97.9 62.9 %copy-start.7 = (f32[32,32,128,1]{2,0,3,1:T(8,128)}, f32[32,32,128,1]{2,0,3,1:T(8,128)S(1)}, u32[]{:S(2)}) copy-start(f32[32,32,128,1]{2,0,3,1:T(8,128)S(1)} %get-tuple-element.44) | copy-start | bytes 1572868
  180.2 6.8 copy-start.28
  180.2 41.7 %all-to-all-start.5 = ((bf16[32,32,8,128]{3,2,0,1:T(8,128)(2,1)}), bf16[32,32,8,128]{3,2,0,1:T(8,128)(2,1)}, u32[]{:S(2)}, u32[]{:S(2)}) async-start(bf16[32,32,8,128]{3,2,0,1:T(8,128)(2,1)} %copy.123), calls=%async_computation.5 | async-start | bytes 4194304 | tf_op jit(solution)/shard_map/all_to_all | solution.py:77
  221.9 118.9 %all-to-all-start = ((bf16[32,32,8,128]{3,0,2,1:T(8,128)(2,1)}), bf16[32,32,8,128]{3,0,2,1:T(8,128)(2,1)}, u32[]{:S(2)}, u32[]{:S(2)}) async-start(bf16[32,32,8,128]{3,0,2,1:T(8,128)(2,1)} %select_bitcast_fusion.3), calls=%async_computation | async-start | bytes 4194304 | tf_op jit(solution)/shard_map/all_to_all | solution.py:46
  230.0 86.6 %copy-start.5 = (bf16[32,4096]{1,0:T(8,128)(2,1)}, bf16[32,4096]{1,0:T(8,128)(2,1)S(1)}, u32[]{:S(2)}) copy-start(bf16[32,4096]{1,0:T(8,128)(2,1)S(1)} %gather_fusion.5) | copy-start | bytes 786436
  233.2 88.2 %copy-start.9 = (f32[32,32,128,1]{2,0,3,1:T(8,128)}, f32[32,32,128,1]{2,0,3,1:T(8,128)S(1)}, u32[]{:S(2)}) copy-start(f32[32,32,128,1]{2,0,3,1:T(8,128)S(1)} %get-tuple-element.46) | copy-start | bytes 1572868
  340.8 36.8 %all-to-all-start.6 = ((bf16[32,32,8,128]{3,2,0,1:T(8,128)(2,1)}), bf16[32,32,8,128]{3,2,0,1:T(8,128)(2,1)}, u32[]{:S(2)}, u32[]{:S(2)}) async-start(bf16[32,32,8,128]{3,2,0,1:T(8,128)(2,1)} %copy.127), calls=%async_computation.6 | async-start | bytes 4194304 | tf_op jit(solution)/shard_map/all_to_all | solution.py:77
  350.4 150.2 %copy-start.18 = (bf16[32,4096]{1,0:T(8,128)(2,1)}, bf16[32,4096]{1,0:T(8,128)(2,1)S(1)}, u32[]{:S(2)}) copy-start(bf16[32,4096]{1,0:T(8,128)(2,1)S(1)} %gather_fusion.6) | copy-start | bytes 786436
  380.7 122.3 %copy-start.25 = (f32[32,32,128,1]{2,0,3,1:T(8,128)}, f32[32,32,128,1]{2,0,3,1:T(8,128)S(1)}, u32[]{:S(2)}) copy-start(f32[32,32,128,1]{2,0,3,1:T(8,128)S(1)} %get-tuple-element.48) | copy-start | bytes 1572868
  539.7 3.0 copy-start.6
  611.6 5.4 copy-start.27
  611.6 33.6 %all-to-all-start.2 = ((bf16[32,32,8,128]{3,0,2,1:T(8,128)(2,1)}), bf16[32,32,8,128]{3,0,2,1:T(8,128)(2,1)}, u32[]{:S(2)}, u32[]{:S(2)}) async-start(bf16[32,32,8,128]{3,0,2,1:T(8,128)(2,1)} %select_bitcast_fusion.1), calls=%async_computation.2 | async-start | bytes 4194304 | tf_op jit(solution)/shard_map/all_to_all | solution.py:46
  645.2 95.1 %all-to-all-start.7 = ((bf16[32,32,8,128]{3,2,0,1:T(8,128)(2,1)}), bf16[32,32,8,128]{3,2,0,1:T(8,128)(2,1)}, u32[]{:S(2)}, u32[]{:S(2)}) async-start(bf16[32,32,8,128]{3,2,0,1:T(8,128)(2,1)} %copy.131), calls=%async_computation.8 | async-start | bytes 4194304 | tf_op jit(solution)/shard_map/all_to_all | solution.py:77
  655.7 4.1 copy-start.8
  740.3 39.0 %all-to-all-start.3 = ((bf16[32,32,8,128]{3,0,2,1:T(8,128)(2,1)}), bf16[32,32,8,128]{3,0,2,1:T(8,128)(2,1)}, u32[]{:S(2)}, u32[]{:S(2)}) async-start(bf16[32,32,8,128]{3,0,2,1:T(8,128)(2,1)} %select_bitcast_fusion), calls=%async_computation.3 | async-start | bytes 4194304 | tf_op jit(solution)/shard_map/all_to_all | solution.py:46
  750.7 274.2 %reduce-scatter.2.cloned.1.call-start = ((), (), s32[]{:S(2)}) async-start(), calls=%async_computation.9 | async-start | bytes 9437184 | tf_op jit(solution)/shard_map/reduce_scatter | solution.py:84
  782.8 3.3 copy-start.12
  782.8 3.3 copy-start.23
  786.2 65.6 %copy-start.19 = (bf16[32,4096]{1,0:T(8,128)(2,1)S(1)}, bf16[32,4096]{1,0:T(8,128)(2,1)}, u32[]{:S(2)}) copy-start(bf16[32,4096]{1,0:T(8,128)(2,1)} %copy-done.18) | copy-start | bytes 786436
  853.5 4.6 copy-start.3
  862.6 4.6 copy-start.2
  880.4 144.6 %copy-start.1 = (bf16[256,4096]{1,0:T(8,128)(2,1)S(1)}, bf16[256,4096]{1,0:T(8,128)(2,1)}, u32[]{:S(2)}) copy-start(bf16[256,4096]{1,0:T(8,128)(2,1)} %param.13) | copy-start | bytes 6291460
  (15 other events, 23.8 us)
Sparse Core Ops, SparseCore 0:
  880.5 144.3 reduce-scatter.1
where the time goes:
time: 1040 us; the launch traced here: 1030 us
  blocking collectives  490 us (47%)
  waiting for transfers between devices  266 us (26%)
  local copies, waits for them, and re-layouts  109 us (10%)
  matrix products  70.2 us (7%)
  starting transfers between devices  58 us (6%)
  other arithmetic  23.4 us (2%)
  between operations  15.1 us (1%)
    psum x3, blocking collectives, shards(): factor = lax.psum(jnp.sum(raw_beta, axis=1), 'state') / states_total  204 us
    psum x3, blocking collectives, shards(): factor = lax.psum(jnp.sum(scaled, axis=1), 'state') / states_total  192 us
    reduce_scatter x1, waiting for transfers between devices, shards(): shares = lax.psum_scatter(counts, 'seq', scatter_dimension=2, tiled=True)  142 us
    all_to_all x4, waiting for transfers between devices, shards(): lax.all_to_all(parcel, 'state', split_axis=1, concat_axis=1, tiled=True)  97 us
    scatter x8, local copies, waits for them, and re-layouts, shards(): parcel = parcel.at[:, own_owner, own_slot].set(partial_value)  72.3 us
    psum x1, blocking collectives, shards(): lax.psum(jnp.sum(scaled * backward, axis=1), 'state') / states_total  62.3 us
    all_to_all x4, starting transfers between devices, shards(): lax.all_to_all(parcel, 'state', split_axis=1, concat_axis=1, tiled=True)  34.8 us
    all_to_all x1, blocking collectives, shards(): lax.all_to_all(fetch_parcel, 'state', split_axis=1, concat_axis=1, tiled=...  32.4 us
  transfers between devices with their start and end apart: 8, of which 6 were waited for; matrix products, arithmetic and copies ran while one was open for 8% of the time, Pallas kernels for 0%

commit v1 on v0

--- a/solution.py
+++ b/solution.py
@@ -36,38 +36,29 @@
         (send_index[:, :, None] == jnp.arange(blocks, dtype=jnp.int32)[None, None, :])
         & filled[:, :, None]
     ).astype(jnp.bfloat16)
+    emissions = [
+        jnp.take(emission_cols, token_ids[:, position], axis=0).astype(jnp.float32)
+        for position in range(STEPS)
+    ]
     forward = alpha_in
-    loglik = jnp.zeros((seq_count,), jnp.float32)
-    stored = []
-    for position in range(STEPS):
-        emission = jnp.take(emission_cols, token_ids[:, position], axis=0).astype(jnp.float32)
+    backward = beta_in
+    fetched_all = [None] * STEPS
+    weighted_all = [None] * STEPS
+    for step in range(STEPS):
         outgoing = forward.astype(jnp.bfloat16)
         fetch_parcel = jnp.take(outgoing.reshape(seq_count, blocks, block_size), send_index, axis=1)
         arrived = lax.all_to_all(fetch_parcel, "state", split_axis=1, concat_axis=1, tiled=True)
         fetched = arrived[:, own_owner, own_slot].reshape(seq_count, blocks, K, block_size)
+        fetched_all[step] = fetched
         mixture = jnp.einsum(
             "sjka,jkab->sjb", fetched, transitions, preferred_element_type=jnp.float32
         ).reshape(seq_count, local_width)
-        scaled = emission * mixture
-        factor = lax.psum(jnp.sum(scaled, axis=1), "state") / states_total
-        loglik = loglik + jnp.log(factor)
-        stored.append((fetched, emission, scaled))
-        forward = scaled / factor[:, None]
-    backward = beta_in
-    counts = jnp.zeros((blocks, K, block_size, block_size), jnp.float32)
-    for position in reversed(range(STEPS)):
-        fetched, emission, scaled = stored[position]
-        weighted = emission * backward
-        pair_mean = lax.psum(jnp.sum(scaled * backward, axis=1), "state") / states_total
-        posterior = (
-            (weighted / pair_mean[:, None])
-            .astype(jnp.bfloat16)
-            .reshape(seq_count, blocks, block_size)
-        )
-        counts = counts + jnp.einsum(
-            "sjka,sjb->jkab", fetched, posterior, preferred_element_type=jnp.float32
-        )
-        spread = weighted.astype(jnp.bfloat16).reshape(seq_count, blocks, block_size)
+        forward = emissions[step] * mixture
+
+        position = STEPS - 1 - step
+        weighted = (emissions[position] * backward).astype(jnp.bfloat16)
+        spread = weighted.reshape(seq_count, blocks, block_size)
+        weighted_all[position] = spread
         partial_value = jnp.einsum(
             "sjb,jkab->sjka", spread, transitions, preferred_element_type=jnp.float32
         )
@@ -75,14 +66,26 @@
         parcel = jnp.zeros((seq_count, peer_count, capacity, block_size), jnp.bfloat16)
         parcel = parcel.at[:, own_owner, own_slot].set(partial_value)
         returned = lax.all_to_all(parcel, "state", split_axis=1, concat_axis=1, tiled=True)
-        raw_beta = jnp.einsum(
+        backward = jnp.einsum(
             "sxca,xcb->sba", returned, collect, preferred_element_type=jnp.float32
         ).reshape(seq_count, local_width)
-        factor = lax.psum(jnp.sum(raw_beta, axis=1), "state") / states_total
-        backward = raw_beta / factor[:, None]
+    ends = jnp.stack([jnp.sum(forward, axis=1), jnp.sum(forward * beta_in, axis=1)])
+    ends = lax.psum(ends, "state") / states_total
+    back_mean = lax.psum(jnp.sum(partial_value.astype(jnp.float32), axis=(1, 2)), "state") / states_total
+    pair = ends[1]
+    fetched = jnp.concatenate(fetched_all, axis=0)
+    posterior = jnp.concatenate(
+        [(w / pair[:, None, None]).astype(jnp.bfloat16) for w in weighted_all], axis=0
+    )
+    counts = jnp.einsum("sjka,sjb->jkab", fetched, posterior, preferred_element_type=jnp.float32)
     counts = counts * transitions.astype(jnp.float32)
     shares = lax.psum_scatter(counts, "seq", scatter_dimension=2, tiled=True)
-    return (shares, forward, backward, loglik)
+    return (
+        shares,
+        forward / ends[0][:, None],
+        backward / back_mean[:, None],
+        jnp.log(ends[0]),
+    )
 
 
 def solution(mesh):

time: 1040 us -> 652 us (0.63)
  blocking collectives: 490 us -> 114 us
  waiting for transfers between devices: 266 us -> 308 us
  matrix products: 70.2 us -> 44.5 us
  local copies, waits for them, and re-layouts: 109 us -> 87.4 us
    psum x7 -> x1, blocking collectives: 458 us -> 60.4 us  [shards(): ends = lax.psum(ends, 'state') / states_total]
    all_to_all x3 -> x4, waiting for transfers between devices: 27 us -> 181 us  [shards(): lax.all_to_all(fetch_parcel, 'state', split_axis=1, concat_axis=1, tiled=...]
    reduce_scatter x1, waiting for transfers between devices: 142 us -> 20 us  [shards(): shares = lax.psum_scatter(counts, 'seq', scatter_dimension=2, tiled=True)]
    scatter x8, local copies, waits for them, and re-layouts: 72.3 us -> 43.1 us  [shards(): parcel = parcel.at[:, own_owner, own_slot].set(partial_value)]
    all_to_all x1, blocking collectives: 32.4 us -> 54.1 us  [shards(): lax.all_to_all(parcel, 'state', split_axis=1, concat_axis=1, tiled=True)]
    all_to_all x4 -> x3, starting transfers between devices: 34.8 us -> 19.3 us  [shards(): lax.all_to_all(parcel, 'state', split_axis=1, concat_axis=1, tiled=True)]
    dot_general x4 -> x1, matrix products: 26.8 us -> 12 us  [shards(): jnp.einsum('sjka,sjb->jkab', fetched, posterior, preferred_element_type=j...]
    gather x4 -> x8, local copies, waits for them, and re-layouts: 12 us -> 24.5 us  [shards(): arrived[:, own_owner, own_slot].reshape(seq_count, blocks, K, block_size)]
  transfers between devices with their start and end apart: 8 -> 8, of which waited for: 6 -> 8; matrix products, arithmetic and copies ran while one was open for 8% -> 5% of each run, Pallas kernels for 0% -> 0%
where the time goes in v1:
time: 652 us; the launch traced here: 643 us
  waiting for transfers between devices  308 us (47%)
  blocking collectives  114 us (17%)
  local copies, waits for them, and re-layouts  87.4 us (13%)
  starting transfers between devices  53.8 us (8%)
  matrix products  44.5 us (7%)
  other arithmetic  20.6 us (3%)
  between operations  14.9 us (2%)
    all_to_all x4, waiting for transfers between devices, shards(): lax.all_to_all(fetch_parcel, 'state', split_axis=1, concat_axis=1, tiled=...  181 us
    all_to_all x3, waiting for transfers between devices, shards(): lax.all_to_all(parcel, 'state', split_axis=1, concat_axis=1, tiled=True)  107 us
    psum x1, blocking collectives, shards(): ends = lax.psum(ends, 'state') / states_total  60.4 us
    all_to_all x1, blocking collectives, shards(): lax.all_to_all(parcel, 'state', split_axis=1, concat_axis=1, tiled=True)  54.1 us
    scatter x8, local copies, waits for them, and re-layouts, shards(): parcel = parcel.at[:, own_owner, own_slot].set(partial_value)  43.1 us
    all_to_all x4, starting transfers between devices, shards(): lax.all_to_all(fetch_parcel, 'state', split_axis=1, concat_axis=1, tiled=...  34.5 us
    gather x8, local copies, waits for them, and re-layouts, shards(): arrived[:, own_owner, own_slot].reshape(seq_count, blocks, K, block_size)  24.5 us
    reduce_scatter x1, waiting for transfers between devices, shards(): shares = lax.psum_scatter(counts, 'seq', scatter_dimension=2, tiled=True)  20 us
  transfers between devices with their start and end apart: 8, of which 8 were waited for; matrix products, arithmetic and copies ran while one was open for 5% of the time, Pallas kernels for 0%

profile of v1, /device:TPU:1, one launch (start us, length us, event | category | flops | bytes accessed | tf_op | source)
XLA Modules:
  0.0 643.5 jit_solution(7653181289469839134)
XLA Ops:
  15.6 12.3 %all-to-all-start = ((bf16[32,32,8,128]{3,0,2,1:T(8,128)(2,1)}), bf16[32,32,8,128]{3,0,2,1:T(8,128)(2,1)}, u32[]{:S(2)}, u32[]{:S(2)}) async-start(bf16[32,32,8,128]{3,0,2,1:T(8,128)(2,1)} %select_bitcast_fusion.3), calls=%async_computation | async-start | bytes 4194304 | tf_op jit(solution)/shard_map/all_to_all | solution.py:50
  30.7 45.7 %all-to-all-done = bf16[32,32,8,128]{3,0,2,1:T(8,128)(2,1)} async-done(((bf16[32,32,8,128]{3,0,2,1:T(8,128)(2,1)}), bf16[32,32,8,128]{3,0,2,1:T(8,128)(2,1)}, u32[]{:S(2)}, u32[]{:S(2)}) %all-to-all-start) | async-done | bytes 2097184 | tf_op jit(solution)/shard_map/all_to_all | solution.py:50
  87.0 6.7 %all-to-all-start.1 = ((bf16[32,32,8,128]{3,0,2,1:T(8,128)(2,1)}), bf16[32,32,8,128]{3,0,2,1:T(8,128)(2,1)}, u32[]{:S(2)}, u32[]{:S(2)}) async-start(bf16[32,32,8,128]{3,0,2,1:T(8,128)(2,1)} %select_bitcast_fusion.2), calls=%async_computation.1 | async-start | bytes 4194304 | tf_op jit(solution)/shard_map/all_to_all | solution.py:50
  95.2 45.7 %all-to-all-done.1 = bf16[32,32,8,128]{3,0,2,1:T(8,128)(2,1)} async-done(((bf16[32,32,8,128]{3,0,2,1:T(8,128)(2,1)}), bf16[32,32,8,128]{3,0,2,1:T(8,128)(2,1)}, u32[]{:S(2)}, u32[]{:S(2)}) %all-to-all-start.1) | async-done | bytes 2097184 | tf_op jit(solution)/shard_map/all_to_all | solution.py:50
  140.9 3.4 gather_fusion.1
  152.7 7.4 %all-to-all-start.2 = ((bf16[32,32,8,128]{3,0,2,1:T(8,128)(2,1)}), bf16[32,32,8,128]{3,0,2,1:T(8,128)(2,1)}, u32[]{:S(2)}, u32[]{:S(2)}) async-start(bf16[32,32,8,128]{3,0,2,1:T(8,128)(2,1)} %select_bitcast_fusion.1), calls=%async_computation.2 | async-start | bytes 4194304 | tf_op jit(solution)/shard_map/all_to_all | solution.py:50
  161.6 44.6 %all-to-all-done.2 = bf16[32,32,8,128]{3,0,2,1:T(8,128)(2,1)} async-done(((bf16[32,32,8,128]{3,0,2,1:T(8,128)(2,1)}), bf16[32,32,8,128]{3,0,2,1:T(8,128)(2,1)}, u32[]{:S(2)}, u32[]{:S(2)}) %all-to-all-start.2) | async-done | bytes 2097184 | tf_op jit(solution)/shard_map/all_to_all | solution.py:50
  206.2 3.5 gather_fusion.2
  218.0 8.0 %all-to-all-start.3 = ((bf16[32,32,8,128]{3,0,2,1:T(8,128)(2,1)}), bf16[32,32,8,128]{3,0,2,1:T(8,128)(2,1)}, u32[]{:S(2)}, u32[]{:S(2)}) async-start(bf16[32,32,8,128]{3,0,2,1:T(8,128)(2,1)} %select_bitcast_fusion), calls=%async_computation.3 | async-start | bytes 4194304 | tf_op jit(solution)/shard_map/all_to_all | solution.py:50
  226.7 45.1 %all-to-all-done.3 = bf16[32,32,8,128]{3,0,2,1:T(8,128)(2,1)} async-done(((bf16[32,32,8,128]{3,0,2,1:T(8,128)(2,1)}), bf16[32,32,8,128]{3,0,2,1:T(8,128)(2,1)}, u32[]{:S(2)}, u32[]{:S(2)}) %all-to-all-start.3) | async-done | bytes 2097184 | tf_op jit(solution)/shard_map/all_to_all | solution.py:50
  281.8 9.8 %scatter_fusion = bf16[32,32,8,128]{3,0,2,1:T(8,128)(2,1)S(1)} fusion(bf16[32,32,8,128]{3,0,2,1:T(8,128)(2,1)S(1)} %broadcast.248.clone.2, s32[128]{0:T(128)S(1)} %get-tuple-element.10, bf16[128,32,128]{2,1,0:T(8,128)(2,1)} %bitcast.276), kind=kCustom, calls=%fused_computation.12 | custom fusion | bytes 3146752 | tf_op jit(solution)/shard_map/scatter | solution.py:67
  293.9 7.7 %all-to-all-start.4 = ((bf16[32,32,8,128]{3,2,0,1:T(8,128)(2,1)}), bf16[32,32,8,128]{3,2,0,1:T(8,128)(2,1)}, u32[]{:S(2)}, u32[]{:S(2)}) async-start(bf16[32,32,8,128]{3,2,0,1:T(8,128)(2,1)} %copy.144), calls=%async_computation.4 | async-start | bytes 4194304 | tf_op jit(solution)/shard_map/all_to_all | solution.py:68
  302.3 44.9 %all-to-all-done.4 = bf16[32,32,8,128]{3,2,0,1:T(8,128)(2,1)} async-done(((bf16[32,32,8,128]{3,2,0,1:T(8,128)(2,1)}), bf16[32,32,8,128]{3,2,0,1:T(8,128)(2,1)}, u32[]{:S(2)}, u32[]{:S(2)}) %all-to-all-start.4) | async-done | bytes 2097184 | tf_op jit(solution)/shard_map/all_to_all | solution.py:68
  353.7 9.8 %scatter_fusion.1 = bf16[32,32,8,128]{3,0,2,1:T(8,128)(2,1)S(1)} fusion(bf16[32,32,8,128]{3,0,2,1:T(8,128)(2,1)S(1)} %broadcast.248.clone.1, s32[128]{0:T(128)S(1)} %get-tuple-element.10, bf16[128,32,128]{2,1,0:T(8,128)(2,1)} %bitcast.277), kind=kCustom, calls=%fused_computation.13 | custom fusion | bytes 3146752 | tf_op jit(solution)/shard_map/scatter | solution.py:67
  364.5 54.1 %all_to_all.40 = bf16[32,32,8,128]{3,2,0,1:T(8,128)(2,1)S(1)} all-to-all(bf16[32,32,8,128]{3,2,0,1:T(8,128)(2,1)S(1)} %copy.147), channel_id=1, replica_groups=mesh['seq'=8,'state'=32] {'state'}, dimensions={1} | all-to-all | bytes 4194304 | tf_op jit(solution)/shard_map/all_to_all | solution.py:68
  423.8 9.8 %scatter_fusion.2 = bf16[32,32,8,128]{3,0,2,1:T(8,128)(2,1)S(1)} fusion(bf16[32,32,8,128]{3,0,2,1:T(8,128)(2,1)S(1)} %broadcast.248.clone, s32[128]{0:T(128)S(1)} %get-tuple-element.10, bf16[128,32,128]{2,1,0:T(8,128)(2,1)} %bitcast.278), kind=kCustom, calls=%fused_computation.14 | custom fusion | bytes 3146752 | tf_op jit(solution)/shard_map/scatter | solution.py:67
  435.9 6.8 %all-to-all-start.6 = ((bf16[32,32,8,128]{3,2,0,1:T(8,128)(2,1)}), bf16[32,32,8,128]{3,2,0,1:T(8,128)(2,1)}, u32[]{:S(2)}, u32[]{:S(2)}) async-start(bf16[32,32,8,128]{3,2,0,1:T(8,128)(2,1)} %copy.150), calls=%async_computation.6 | async-start | bytes 4194304 | tf_op jit(solution)/shard_map/all_to_all | solution.py:68
  455.3 32.2 %all-to-all-done.6 = bf16[32,32,8,128]{3,2,0,1:T(8,128)(2,1)} async-done(((bf16[32,32,8,128]{3,2,0,1:T(8,128)(2,1)}), bf16[32,32,8,128]{3,2,0,1:T(8,128)(2,1)}, u32[]{:S(2)}, u32[]{:S(2)}) %all-to-all-start.6) | async-done | bytes 2097184 | tf_op jit(solution)/shard_map/all_to_all | solution.py:68
  493.1 60.4 %all-reduce = (f32[2,32]{1,0:T(2,128)S(1)}, f32[32]{0:T(128)S(1)}) all-reduce(f32[2,32]{1,0:T(2,128)S(1)} %pad_maximum_fusion, f32[32]{0:T(128)S(1)} %get-tuple-element.38), channel_id=1, replica_groups=mesh['seq'=8,'state'=32] {'state'}, use_global_device_ids=true, to_apply=%region_9.12 | all-reduce | flops 96 | bytes 768 | tf_op jit(solution)/shard_map/psum | solution.py:73
  555.6 12.0 %convert_multiply_fusion = f32[32,4,128,128]{3,2,1,0:T(8,128)} fusion(bf16[32,4,128,128]{3,2,1,0:T(8,128)(2,1)} %param.12, bf16[32,32,4,128]{0,3,2,1:T(8,128)(2,1)} %bitcast.262, bf16[32,32,4,128]{0,3,2,1:T(8,128)(2,1)} %bitcast.261, bf16[32,32,4,128]{0,3,2,1:T(8,128)(2,1)} %bitcast.260, bf16[32,32,4,128]{0,3,2,1:T(8,128)(2,1)} %bitcast.259, ...), kind=kOutput, calls=%fused_computation.16 | convolution fusion | flops 562036736 | bytes 17825792 | tf_op jit(solution)/shard_map/sjka,sjb->jkab/dot_general | solution.py:80
  568.1 5.9 scatter_fusion.3
  576.4 4.9 all-to-all-start.7
  582.7 29.6 %all-to-all-done.7 = bf16[32,32,8,128]{3,2,0,1:T(8,128)(2,1)} async-done(((bf16[32,32,8,128]{3,2,0,1:T(8,128)(2,1)}), bf16[32,32,8,128]{3,2,0,1:T(8,128)(2,1)}, u32[]{:S(2)}, u32[]{:S(2)}) %all-to-all-start.7) | async-done | bytes 2097184 | tf_op jit(solution)/shard_map/all_to_all | solution.py:68
  616.4 20.0 %reduce-scatter.2.cloned.1.call-done = f32[32,4,16,128]{3,2,1,0:T(8,128)} async-done(((f32[32,4,128,128]{3,2,1,0:T(8,128)}), f32[32,4,16,128]{3,2,1,0:T(8,128)}) %reduce-scatter.2.cloned.1.call-update) | async-done | bytes 1048592 | tf_op jit(solution)/shard_map/reduce_scatter | solution.py:82
  (146 shorter events, 98.4 us)
Async XLA Ops:
  7.2 21.9 %copy-start = (bf16[256,4096]{1,0:T(8,128)(2,1)S(1)}, bf16[256,4096]{1,0:T(8,128)(2,1)}, u32[]{:S(2)}) copy-start(bf16[256,4096]{1,0:T(8,128)(2,1)} %param.13) | copy-start | bytes 6291460
  15.6 13.4 %copy-start.29 = (s32[32,4]{0,1:T(4,128)S(1)}, s32[32,4]{0,1:T(4,128)}, u32[]{:S(2)}) copy-start(s32[32,4]{0,1:T(4,128)} %param.14) | copy-start | bytes 1540
  15.6 60.8 %all-to-all-start = ((bf16[32,32,8,128]{3,0,2,1:T(8,128)(2,1)}), bf16[32,32,8,128]{3,0,2,1:T(8,128)(2,1)}, u32[]{:S(2)}, u32[]{:S(2)}) async-start(bf16[32,32,8,128]{3,0,2,1:T(8,128)(2,1)} %select_bitcast_fusion.3), calls=%async_computation | async-start | bytes 4194304 | tf_op jit(solution)/shard_map/all_to_all | solution.py:50
  87.0 53.9 %all-to-all-start.1 = ((bf16[32,32,8,128]{3,0,2,1:T(8,128)(2,1)}), bf16[32,32,8,128]{3,0,2,1:T(8,128)(2,1)}, u32[]{:S(2)}, u32[]{:S(2)}) async-start(bf16[32,32,8,128]{3,0,2,1:T(8,128)(2,1)} %select_bitcast_fusion.2), calls=%async_computation.1 | async-start | bytes 4194304 | tf_op jit(solution)/shard_map/all_to_all | solution.py:50
  152.7 53.5 %all-to-all-start.2 = ((bf16[32,32,8,128]{3,0,2,1:T(8,128)(2,1)}), bf16[32,32,8,128]{3,0,2,1:T(8,128)(2,1)}, u32[]{:S(2)}, u32[]{:S(2)}) async-start(bf16[32,32,8,128]{3,0,2,1:T(8,128)(2,1)} %select_bitcast_fusion.1), calls=%async_computation.2 | async-start | bytes 4194304 | tf_op jit(solution)/shard_map/all_to_all | solution.py:50
  218.0 53.8 %all-to-all-start.3 = ((bf16[32,32,8,128]{3,0,2,1:T(8,128)(2,1)}), bf16[32,32,8,128]{3,0,2,1:T(8,128)(2,1)}, u32[]{:S(2)}, u32[]{:S(2)}) async-start(bf16[32,32,8,128]{3,0,2,1:T(8,128)(2,1)} %select_bitcast_fusion), calls=%async_computation.3 | async-start | bytes 4194304 | tf_op jit(solution)/shard_map/all_to_all | solution.py:50
  226.7 51.0 %copy-start.20 = (bf16[32,4096]{1,0:T(8,128)(2,1)}, bf16[32,4096]{1,0:T(8,128)(2,1)S(1)}, u32[]{:S(2)}) copy-start(bf16[32,4096]{1,0:T(8,128)(2,1)S(1)} %gather_fusion.11) | copy-start | bytes 786436
  274.3 4.4 copy-start.2
  293.9 53.3 %all-to-all-start.4 = ((bf16[32,32,8,128]{3,2,0,1:T(8,128)(2,1)}), bf16[32,32,8,128]{3,2,0,1:T(8,128)(2,1)}, u32[]{:S(2)}, u32[]{:S(2)}) async-start(bf16[32,32,8,128]{3,2,0,1:T(8,128)(2,1)} %copy.144), calls=%async_computation.4 | async-start | bytes 4194304 | tf_op jit(solution)/shard_map/all_to_all | solution.py:68
  301.6 48.7 %copy-start.18 = (bf16[32,4096]{1,0:T(8,128)(2,1)S(1)}, bf16[32,4096]{1,0:T(8,128)(2,1)}, u32[]{:S(2)}) copy-start(bf16[32,4096]{1,0:T(8,128)(2,1)} %gather_fusion.9) | copy-start | bytes 786436
  364.5 55.4 %copy-start.15 = (bf16[32,4096]{1,0:T(8,128)(2,1)S(1)}, bf16[32,4096]{1,0:T(8,128)(2,1)}, u32[]{:S(2)}) copy-start(bf16[32,4096]{1,0:T(8,128)(2,1)} %gather_fusion.7) | copy-start | bytes 786436
  435.9 51.6 %all-to-all-start.6 = ((bf16[32,32,8,128]{3,2,0,1:T(8,128)(2,1)}), bf16[32,32,8,128]{3,2,0,1:T(8,128)(2,1)}, u32[]{:S(2)}, u32[]{:S(2)}) async-start(bf16[32,32,8,128]{3,2,0,1:T(8,128)(2,1)} %copy.150), calls=%async_computation.6 | async-start | bytes 4194304 | tf_op jit(solution)/shard_map/all_to_all | solution.py:68
  442.7 193.7 %reduce-scatter.2.cloned.1.call-start = ((), (), s32[]{:S(2)}) async-start(), calls=%async_computation.9 | async-start | bytes 9437184 | tf_op jit(solution)/shard_map/reduce_scatter | solution.py:82
  455.3 35.3 %copy-start.13 = (bf16[32,4096]{1,0:T(8,128)(2,1)S(1)}, bf16[32,4096]{1,0:T(8,128)(2,1)}, u32[]{:S(2)}) copy-start(bf16[32,4096]{1,0:T(8,128)(2,1)} %gather_fusion.5) | copy-start | bytes 786436
  487.5 3.9 copy-start.5
  491.4 62.1 %copy-start.16 = (bf16[32,4096]{1,0:T(8,128)(2,1)S(1)}, bf16[32,4096]{1,0:T(8,128)(2,1)}, u32[]{:S(2)}) copy-start(bf16[32,4096]{1,0:T(8,128)(2,1)} %gather_fusion.7) | copy-start | bytes 786436
  491.4 62.1 %copy-start.19 = (bf16[32,4096]{1,0:T(8,128)(2,1)S(1)}, bf16[32,4096]{1,0:T(8,128)(2,1)}, u32[]{:S(2)}) copy-start(bf16[32,4096]{1,0:T(8,128)(2,1)} %gather_fusion.9) | copy-start | bytes 786436
  491.4 62.1 %copy-start.23 = (f32[32,32,128,1]{2,0,3,1:T(8,128)S(1)}, f32[32,32,128,1]{2,0,3,1:T(8,128)}, u32[]{:S(2)}) copy-start(f32[32,32,128,1]{2,0,3,1:T(8,128)} %copy-done.22) | copy-start | bytes 1572868
  491.4 62.1 %copy-start.25 = (f32[32,32,128,1]{2,0,3,1:T(8,128)S(1)}, f32[32,32,128,1]{2,0,3,1:T(8,128)}, u32[]{:S(2)}) copy-start(f32[32,32,128,1]{2,0,3,1:T(8,128)} %copy-done.24) | copy-start | bytes 1572868
  491.4 62.1 %copy-start.27 = (bf16[4,32,8,128]{3,2,1,0:T(8,128)(2,1)S(1)}, bf16[4,32,8,128]{3,2,1,0:T(8,128)(2,1)}, u32[]{:S(2)}) copy-start(bf16[4,32,8,128]{3,2,1,0:T(8,128)(2,1)} %get-tuple-element.23) | copy-start | bytes 786436
  576.4 5.4 copy-start.11
  576.4 5.4 copy-start.21
  576.4 36.0 %all-to-all-start.7 = ((bf16[32,32,8,128]{3,2,0,1:T(8,128)(2,1)}), bf16[32,32,8,128]{3,2,0,1:T(8,128)(2,1)}, u32[]{:S(2)}, u32[]{:S(2)}) async-start(bf16[32,32,8,128]{3,2,0,1:T(8,128)(2,1)} %copy.159), calls=%async_computation.8 | async-start | bytes 4194304 | tf_op jit(solution)/shard_map/all_to_all | solution.py:68
  581.8 54.6 %copy-start.1 = (bf16[256,4096]{1,0:T(8,128)(2,1)S(1)}, bf16[256,4096]{1,0:T(8,128)(2,1)}, u32[]{:S(2)}) copy-start(bf16[256,4096]{1,0:T(8,128)(2,1)} %param.13) | copy-start | bytes 6291460
  (14 other events, 42.2 us)
Sparse Core Ops, SparseCore 0:
  567.8 68.5 reduce-scatter.1

commit v2 on v0

v2 whole, which is shorter than its diff:
```python
import functools

import jax
import jax.numpy as jnp
from jax import lax
from jax.experimental import pallas as pl
from jax.experimental.pallas import tpu as pltpu
from jax.sharding import PartitionSpec as P

K = 4
STEPS = 4
NZ = 8
NY = 4
CAP = 8
NB = 32
NS = 32
BS = 128
REFS = NB * K
COL = NZ * CAP
CHUNK = 8
MESH = pl.DeviceIdType.MESH
F32 = jnp.float32
BF16 = jnp.bfloat16

SEL, REF, INV, ORD, LO, HI = 0, 256, 384, 640, 896, 1152


def index_tables(sources):
    rank = lax.axis_index("state")
    z, y = rank // NY, rank % NY
    rows = lax.dynamic_slice_in_dim(sources.reshape(NZ, NY * REFS), z, 1, 0).reshape(NY, REFS)
    rows = jnp.roll(rows, -y, axis=0)
    owner, local = rows // NB, rows % NB
    ordinal = jnp.arange(REFS, dtype=jnp.int32)
    earlier = (owner[:, None, :] == owner[:, :, None]) & (ordinal[None, :] < ordinal[:, None])[None]
    slot = jnp.sum(earlier.astype(jnp.int32), axis=2)
    place = (owner // NY) * CAP + slot
    column = owner % NY
    spots = jnp.arange(COL, dtype=jnp.int32)
    mine = (column == y)[:, :, None] & (place[:, :, None] == spots)
    sel = jnp.sum(jnp.where(mine, local[:, :, None], 0), axis=1)
    filled = jnp.any(mine, axis=1)
    ref = ((y - column[0]) % NY) * COL + place[0]
    towards = ((column[0] - y) % NY) * COL + place[0]
    inv = jnp.sum(
        jnp.where(towards[:, None] == jnp.arange(NY * COL, dtype=jnp.int32), ordinal[:, None], 0), axis=0
    )
    key = jnp.where(filled, sel, NB)
    key = jnp.concatenate([key[:1], key[:0:-1]], axis=0).reshape(NY, NZ, CAP)
    key = key.transpose(1, 0, 2).reshape(NZ, NY * CAP)
    number = jnp.arange(NY * CAP, dtype=jnp.int32)
    less = (key[:, None, :] < key[:, :, None]) | (
        (key[:, None, :] == key[:, :, None]) & (number[None, :] < number[:, None])[None]
    )
    rank_of = jnp.sum(less.astype(jnp.int32), axis=2)
    home = (number // CAP) * COL + number % CAP
    home = home[None, :] + jnp.arange(NZ, dtype=jnp.int32)[:, None] * CAP
    order = jnp.sum(jnp.where(rank_of[:, :, None] == number, home[:, :, None], 0), axis=1)
    blocks = jnp.arange(NB, dtype=jnp.int32)
    low = jnp.sum((key[:, None, :] < blocks[None, :, None]).astype(jnp.int32), axis=2)
    high = jnp.sum((key[:, None, :] <= blocks[None, :, None]).astype(jnp.int32), axis=2)
    return jnp.concatenate([part.reshape(-1).astype(jnp.int32) for part in (sel, ref, inv, order, low, high)])


def body(
    tab, alpha, beta, tr, em,
    counts, alpha_end, beta_start, loglik,
    zg0, zg1, yr0, yr1, yr2, yr3, ys, pb, bsend, br0, br1, pre, psv,
    rs_snd, rs_rcv, rl_snd, rl_rcv, w, bacc, cs, cr, sa, sb, sc, sd, scale,
    ag_s, ag_r, bw_s, bw_r, fw_s, fw_r, rs_s, rs_r, sy_s, sy_r, sz_s, sz_r, ct_s, ct_r,
):
    q, p = lax.axis_index("seq"), lax.axis_index("state")
    z, y = p // NY, p % NY
    zgs, yrs, brs = (zg0, zg1), (yr0, yr1, yr2, yr3), (br0, br1)
    total_states = float(NB * BS * NZ * NY)

    def at_z(dz):
        return (q, lax.rem(z + dz + NZ, NZ) * NY + y)

    def at_y(dy):
        return (q, z * NY + lax.rem(y + dy, NY))

    def at_q(dq):
        return (lax.rem(q + dq, 8), p)

    barrier = pltpu.get_barrier_semaphore()
    for dz in range(1, NZ):
        pl.semaphore_signal(barrier, inc=1, device_id=at_z(dz), device_id_type=MESH)
    for dy in range(1, NY):
        pl.semaphore_signal(barrier, inc=1, device_id=at_y(dy), device_id_type=MESH)
    for dq in range(1, 8):
        pl.semaphore_signal(barrier, inc=1, device_id=at_q(dq), device_id_type=MESH)
    pl.semaphore_wait(barrier, NZ - 1 + NY - 1 + 7)

    def remote(src, dst, send, recv, device):
        return pltpu.make_async_remote_copy(
            src_ref=src, dst_ref=dst, send_sem=send, recv_sem=recv, device_id=device, device_id_type=MESH
        )

    def cols(j):
        return pl.ds(pl.multiple_of(j * BS, BS), BS)

    def gather_copy(r, way, h):
        zg = zgs[r % 2]
        near, far = (h - 1, h) if way else ((1 - h) % NZ, (-h) % NZ)
        src, dst = zg.at[near], zg.at[far]
        if h == 4:
            half = pl.ds(way * 16, 16)
            src, dst = zg.at[near, half], zg.at[far, half]
        return remote(src, dst, ag_s.at[r, way, h - 1], ag_r.at[r, way, h - 1], at_z(-1 if way else 1))

    def reduce_copy(r, way, h):
        snd, rcv = (rl_snd, rl_rcv) if r == 3 else (rs_snd, rs_rcv)
        src, dst = snd.at[way, h - 1], rcv.at[way, h - 1]
        if h == 1:
            half = pl.ds(way * 16, 16)
            src, dst = snd.at[way, 0, half], rcv.at[way, 0, half]
        return remote(src, dst, rs_s.at[r, way, h - 1], rs_r.at[r, way, h - 1], at_z(-1 if way else 1))

    def back_copy(r, dy):
        return remote(
            bsend.at[dy - 1], brs[r % 2].at[pl.ds(dy * COL, COL)], bw_s.at[r, dy - 1], bw_r.at[r, dy - 1], at_y(dy)
        )

    def fetch_copy(r, dy):
        return remote(
            ys.at[dy - 1], yrs[r].at[pl.ds(dy * COL, COL)], fw_s.at[r, dy - 1], fw_r.at[r, dy - 1], at_y(dy)
        )

    def sum_y_copy(n, dy):
        return remote(sa.at[n], sb.at[n, dy - 1], sy_s.at[n, dy - 1], sy_r.at[n, dy - 1], at_y(dy))

    def sum_z_copy(n, dz):
        return remote(sc.at[n], sd.at[n, dz - 1], sz_s.at[n, dz - 1], sz_r.at[n, dz - 1], at_z(dz))

    def counts_copy(c, dq):
        piece = pl.ds(c * CHUNK, CHUNK)
        return remote(
            cs.at[lax.rem(q + dq, 8), piece], cr.at[dq - 1, piece], ct_s.at[c, dq - 1], ct_r.at[c, dq - 1], at_q(dq)
        )

    def sum_over_y(n):
        for dy in range(1, NY):
            sum_y_copy(n, dy).start()

    def sum_over_z(n):
        for dy in range(1, NY):
            sum_y_copy(n, dy).wait()
        sc[n] = sa[n] + sb[n, 0] + sb[n, 1] + sb[n, 2]
        for dz in range(1, NZ):
            sum_z_copy(n, dz).start()

    def sum_result(n):
        for dz in range(1, NZ):
            sum_z_copy(n, dz).wait()
        total = sc[n]
        for dz in range(1, NZ):
            total = total + sd[n, dz - 1]
        return jnp.sum(total, axis=2, keepdims=True) / total_states

    def weigh(r):
        u = STEPS - 1 - r

        def step(b, carry):
            message = beta[:, cols(b)] if r == 0 else bacc[b]
            if r == 3:
                message = message * scale[1]
            w[u, b] = (em[u, :, cols(b)].astype(F32) * message).astype(BF16)
            return carry

        lax.fori_loop(0, NB, step, 0)

    def partials(r):
        u = STEPS - 1 - r

        def step(j, acc):
            out = lax.dot_general(w[u, j], tr[j], (((1,), (1,)), ((), ())), preferred_element_type=F32)
            for k in range(K):
                piece = out[:, k * BS : (k + 1) * BS]
                pb[j * K + k] = piece.astype(BF16)
                if r >= 2:
                    acc = acc + piece
            return acc

        return lax.fori_loop(0, NB, step, jnp.zeros((NS, BS), F32))

    def relay(r, d):
        br = brs[r % 2]
        base = lax.rem(z + d + NZ, NZ) * NB
        pre[0] = jnp.zeros((NS, BS), F32)

        def add(i, acc):
            acc = acc + br[tab[ORD + base + i]].astype(F32)
            pre[i + 1] = acc
            return acc

        lax.fori_loop(0, NB, add, jnp.zeros((NS, BS), F32))

        def differ(b, carry):
            psv[d % NZ, b] = pre[tab[HI + base + b]] - pre[tab[LO + base + b]]
            return carry

        lax.fori_loop(0, NB, differ, 0)

    def begin(b, carry):
        zg0[0, b] = alpha[:, cols(b)].astype(BF16)
        return carry

    lax.fori_loop(0, NB, begin, 0)

    for r in range(STEPS):
        zg, yr, br = zgs[r % 2], yrs[r], brs[r % 2]
        for way in range(2):
            gather_copy(r, way, 1).start()
        weigh(r)
        acc = partials(r)
        if r >= 2:
            sa[r - 2, 1] = acc
        if r == 2:
            sum_over_y(0)
        for dy in (1, 3, 2):

            def pack(i, carry, dy=dy):
                bsend[dy - 1, i] = pb[tab[INV + dy * COL + i]]
                return carry

            lax.fori_loop(0, COL, pack, 0)
            back_copy(r, dy).start()

        def keep(i, carry):
            br[i] = pb[tab[INV + i]]
            return carry

        lax.fori_loop(0, COL, keep, 0)
        for h in range(2, 5):
            for way in range(2):
                gather_copy(r, way, h - 1).wait_recv()
                gather_copy(r, way, h).start()
        for way in range(2):
            gather_copy(r, way, 4).wait_recv()

        for dy in (1, 3, 2):

            def choose(i, carry, dy=dy):
                d = lax.rem(i // CAP - z + NZ, NZ)
                ys[dy - 1, i] = zg[d, tab[SEL + dy * COL + i]]
                return carry

            lax.fori_loop(0, COL, choose, 0)
            fetch_copy(r, dy).start()

        def hold(i, carry):
            d = lax.rem(i // CAP - z + NZ, NZ)
            yr[i] = zg[d, tab[SEL + i]]
            return carry

        lax.fori_loop(0, COL, hold, 0)
        for way in range(2):
            for h in range(1, 5):
                gather_copy(r, way, h).wait_send()
        for dy in range(1, NY):
            back_copy(r, dy).wait()
        if r == 2:
            sum_over_z(0)

        snd, rcv = (rl_snd, rl_rcv) if r == 3 else (rs_snd, rs_rcv)
        kind = snd.dtype
        relay(r, 4)

        def far(b, carry):
            snd[0, 0, b] = psv[4, b].astype(kind)
            snd[1, 0, b + 16] = psv[4, b + 16].astype(kind)
            return carry

        lax.fori_loop(0, 16, far, 0)
        for way in range(2):
            reduce_copy(r, way, 1).start()
        for h in range(2, 5):
            d = 5 - h
            relay(r, d)
            relay(r, -d)
            for way in range(2):
                reduce_copy(r, way, h - 1).wait_recv()
                dd = (-d if way else d) % NZ
                if h == 2:

                    def join(b, carry, way=way, dd=dd):
                        there, other = b + way * 16, b + (1 - way) * 16
                        snd[way, 1, there] = (psv[dd, there] + rcv[way, 0, there].astype(F32)).astype(kind)
                        snd[way, 1, other] = psv[dd, other].astype(kind)
                        return carry

                    lax.fori_loop(0, 16, join, 0)
                else:

                    def join(b, carry, way=way, dd=dd, h=h):
                        snd[way, h - 1, b] = (psv[dd, b] + rcv[way, h - 2, b].astype(F32)).astype(kind)
                        return carry

                    lax.fori_loop(0, NB, join, 0)
                reduce_copy(r, way, h).start()
        relay(r, 0)
        if r < 3:
            for way in range(2):
                reduce_copy(r, way, 4).wait_recv()

            def finish(b, carry):
                bacc[b] = psv[0, b] + rcv[0, 3, b].astype(F32) + rcv[1, 3, b].astype(F32)
                return carry

            lax.fori_loop(0, NB, finish, 0)
            for way in range(2):
                for h in range(1, 5):
                    reduce_copy(r, way, h).wait_send()
        if r == 2:
            means = sum_result(0)
            scale[0] = jnp.broadcast_to(1.0 / means[0], (NS, BS))
            scale[1] = jnp.broadcast_to(1.0 / means[1], (NS, BS))
            scale[2] = jnp.broadcast_to(means[1] / means[0], (NS, BS))

        for dy in range(1, NY):
            fetch_copy(r, dy).wait()

        def mix(j, acc):
            x = jnp.concatenate([yr[tab[REF + j * K + k]] for k in range(K)], axis=1)
            value = jnp.dot(x, tr[j], preferred_element_type=F32) * em[r, :, cols(j)].astype(F32)
            if r == 3:
                alpha_end[:, cols(j)] = value
                return acc + value
            zgs[(r + 1) % 2][0, j] = value.astype(BF16)
            if r == 1:
                acc = acc + value * bacc[j]
            return acc

        acc = lax.fori_loop(0, NB, mix, jnp.zeros((NS, BS), F32))
        if r == 1:
            sa[0, 0] = acc
        if r == 3:
            sa[1, 0] = acc
            sum_over_y(1)

    for c in range(NB // CHUNK):

        def tally(i, carry, c=c):
            j = c * CHUNK + i
            x = jnp.concatenate(
                [jnp.concatenate([v[tab[REF + j * K + k]] for k in range(K)], axis=1) for v in yrs], axis=0
            )
            weights = jnp.concatenate(
                [(w[t, j].astype(F32) * scale[2 if t == 0 else 0]).astype(BF16) for t in range(STEPS)], axis=0
            )
            out = lax.dot_general(x, weights, (((0,), (0,)), ((), ())), preferred_element_type=F32).astype(BF16)
            for k in range(K):
                for part in range(8):
                    first = k * BS + part * 16
                    cs[part, j, k] = out[first : first + 16]
            return carry

        lax.fori_loop(0, CHUNK, tally, 0)
        for dq in range(1, 8):
            counts_copy(c, dq).start()
        if c == 0:
            sum_over_z(1)

    for way in range(2):
        reduce_copy(3, way, 4).wait_recv()
    means = sum_result(1)
    start_scale = jnp.broadcast_to(1.0 / means[1], (NS, BS))
    end_scale = jnp.broadcast_to(1.0 / means[0], (NS, BS))
    loglik[...] = jnp.broadcast_to(jnp.log(means[0]), (NS, BS))

    def last(b, carry):
        beta_start[:, cols(b)] = (psv[0, b] + rl_rcv[0, 3, b] + rl_rcv[1, 3, b]) * start_scale
        alpha_end[:, cols(b)] = alpha_end[:, cols(b)] * end_scale
        return carry

    lax.fori_loop(0, NB, last, 0)
    for way in range(2):
        for h in range(1, 5):
            reduce_copy(3, way, h).wait_send()

    for c in range(NB // CHUNK):
        for dq in range(1, 8):
            counts_copy(c, dq).wait()

        def total(i, carry, c=c):
            j = c * CHUNK + i
            value = cs[q, j].astype(F32)
            for dq in range(1, 8):
                value = value + cr[dq - 1, j].astype(F32)
            for k in range(K):
                rows = pl.ds(pl.multiple_of(k * BS + q * 16, 16), 16)
                counts[j, k] = value[k] * tr[j, rows, :].astype(F32)
            return carry

        lax.fori_loop(0, CHUNK, total, 0)


def shards(alpha_in, beta_in, transitions, emission_cols, token_ids, sources):
    tables = index_tables(sources)
    em = jnp.take(emission_cols, token_ids.T, axis=0)
    shard = (NB, NS, BS)
    vmem = pl.BlockSpec(memory_space=pltpu.VMEM)
    dma = pltpu.SemaphoreType.DMA
    out = pl.pallas_call(
        body,
        out_shape=(
            jax.ShapeDtypeStruct((NB, K, BS // 8, BS), F32),
            jax.ShapeDtypeStruct((NS, NB * BS), F32),
            jax.ShapeDtypeStruct((NS, NB * BS), F32),
            jax.ShapeDtypeStruct((NS, BS), F32),
        ),
        in_specs=[pl.BlockSpec(memory_space=pltpu.SMEM)] + [vmem] * 4,
        out_specs=(vmem,) * 4,
        scratch_shapes=[
            pltpu.VMEM((NZ,) + shard, BF16),
            pltpu.VMEM((NZ,) + shard, BF16),
            *[pltpu.VMEM((NY * COL, NS, BS), BF16)] * STEPS,
            pltpu.VMEM((NY - 1, COL, NS, BS), BF16),
            pltpu.VMEM((REFS, NS, BS), BF16),
            pltpu.VMEM((NY - 1, COL, NS, BS), BF16),
            pltpu.VMEM((NY * COL, NS, BS), BF16),
            pltpu.VMEM((NY * COL, NS, BS), BF16),
            pltpu.VMEM((NB + 1, NS, BS), F32),
            pltpu.VMEM((NZ,) + shard, F32),
            pltpu.VMEM((2, 4) + shard, BF16),
            pltpu.VMEM((2, 4) + shard, BF16),
            pltpu.VMEM((2, 4) + shard, F32),
            pltpu.VMEM((2, 4) + shard, F32),
            pltpu.VMEM((STEPS,) + shard, BF16),
            pltpu.VMEM(shard, F32),
            pltpu.VMEM((8, NB, K, BS // 8, BS), BF16),
            pltpu.VMEM((7, NB, K, BS // 8, BS), BF16),
            pltpu.VMEM((2, 2, NS, BS), F32),
            pltpu.VMEM((2, NY - 1, 2, NS, BS), F32),
            pltpu.VMEM((2, 2, NS, BS), F32),
            pltpu.VMEM((2, NZ - 1, 2, NS, BS), F32),
            pltpu.VMEM((3, NS, BS), F32),
            *[dma((STEPS, 2, 4))] * 2,
            *[dma((STEPS, NY - 1))] * 4,
            *[dma((STEPS, 2, 4))] * 2,
            *[dma((2, NY - 1))] * 2,
            *[dma((2, NZ - 1))] * 2,
            *[dma((NB // CHUNK, 7))] * 2,
        ],
        compiler_params=pltpu.CompilerParams(
            collective_id=0, has_side_effects=True, vmem_limit_bytes=62 * 2**20
        ),
        cost_estimate=pl.CostEstimate(flops=1_700_000_000, bytes_accessed=10_000_000, transcendentals=32),
    )(tables, alpha_in, beta_in, transitions.reshape(NB, K * BS, BS), em)
    return out[0], out[1], out[2], out[3][:, 0]


def solution(mesh):
    placed = (
        P("seq", "state"),
        P("seq", "state"),
        P("state", None, None, None),
        P(None, "state"),
        P("seq", None),
        P(),
    )
    return jax.shard_map(
        shards,
        mesh=mesh,
        in_specs=placed,
        out_specs=(P("state", None, "seq", None), P("seq", "state"), P("seq", "state"), P("seq")),
        check_vma=False,
    )
```

time: 1040 us -> 321 us (0.31)
  blocking collectives: 490 us -> 0 us
  Pallas kernels: 0 us -> 304 us
  waiting for transfers between devices: 266 us -> 0 us
  local copies, waits for them, and re-layouts: 109 us -> 11.3 us
  matrix products: 70.2 us -> 0 us
  starting transfers between devices: 58 us -> 0 us
  other arithmetic: 23.4 us -> 4.03 us
  between operations: 15.1 us -> 0.83 us
    psum x7 -> x0, blocking collectives: 458 us -> none  [the longest x3 204 us: shards(): factor = lax.psum(jnp.sum(raw_beta, axis=1), 'state') / states_total]
    pallas_call x0 -> x1, Pallas kernels: none -> 304 us  [shards(): pl.pallas_call(body, out_shape=(jax.ShapeDtypeStruct((NB, K, BS // 8, BS)...]
    reduce_scatter x1 -> x0, waiting for transfers between devices: 142 us -> none  [shards(): shares = lax.psum_scatter(counts, 'seq', scatter_dimension=2, tiled=True)]
    all_to_all x7 -> x0, waiting for transfers between devices: 124 us -> none  [the longest x4 97 us: shards(): lax.all_to_all(parcel, 'state', split_axis=1, concat_axis=1, tiled=True)]
    scatter x8 -> x0, local copies, waits for them, and re-layouts: 72.3 us -> none  [shards(): parcel = parcel.at[:, own_owner, own_slot].set(partial_value)]
    dot_general x16 -> x0, matrix products: 70.2 us -> none  [the longest x4 26.8 us: shards(): jnp.einsum('sjka,sjb->jkab', fetched, posterior, preferred_element_type=j...]
    all_to_all x7 -> x0, starting transfers between devices: 58 us -> none  [the longest x4 34.8 us: shards(): lax.all_to_all(parcel, 'state', split_axis=1, concat_axis=1, tiled=True)]
    all_to_all x1 -> x0, blocking collectives: 32.4 us -> none  [shards(): lax.all_to_all(fetch_parcel, 'state', split_axis=1, concat_axis=1, tiled=...]
  transfers between devices with their start and end apart: 8 -> 0, of which waited for: 6 -> 0; matrix products, arithmetic and copies ran while one was open for 8% -> 0% of each run, Pallas kernels for 0% -> 0%
where the time goes in v2:
time: 321 us; the launch traced here: 320 us
  Pallas kernels  304 us (95%)
  local copies, waits for them, and re-layouts  11.3 us (4%)
  other arithmetic  4.03 us (1%)
    pallas_call x1, Pallas kernels, shards(): pl.pallas_call(body, out_shape=(jax.ShapeDtypeStruct((NB, K, BS // 8, BS)...  304 us

profile of v2, /device:TPU:1, one launch (start us, length us, event | category | flops | bytes accessed | tf_op | source)
XLA Modules:
  0.0 320.4 jit_solution(10654384016628955663)
XLA Ops:
  0.7 0.7 compare_and_fusion
  1.4 0.7 compare_select_fusion
  2.1 0.1 reshape.159
  2.3 0.9 copy.13
  3.2 0.3 reshape.149
  3.5 0.2 convert_reduce_fusion
  3.8 0.1 select_reduce_fusion.2
  4.0 0.2 fusion.1
  4.1 0.1 reshape.151
  4.2 0.1 select_reduce_fusion.1
  4.4 0.1 reshape.152
  4.5 0.1 lt.128
  4.6 0.5 convert_reduce_fusion.1
  5.1 0.1 select_reduce_fusion
  5.3 0.1 reshape.153
  5.4 0.1 reshape.155
  5.4 0.1 reshape.154
  5.5 4.1 %gather_fusion = bf16[128,4096]{1,0:T(8,128)(2,1)S(1)} fusion(bf16[256,4096]{1,0:T(8,128)(2,1)} %param.9, s32[1024]{0:T(1024)S(1)} %pad_clamp_fusion), kind=kCustom, calls=%fused_computation | custom fusion | bytes 2097664 | tf_op jit(solution)/shard_map/jit(_take)/gather | solution.py:401
  9.6 1.1 broadcast_select_fusion.em
  10.8 304.3 %shard_map.93 = (f32[32,4,16,128]{3,2,1,0:T(8,128)}, f32[32,4096]{1,0:T(8,128)}, f32[32,4096]{1,0:T(8,128)}, f32[32,128]{1,0:T(8,128)}) custom-call(s32[1408]{0:T(1024)} %copy-done.2, f32[32,4096]{1,0:T(8,128)} %alpha.1, f32[32,4096]{1,0:T(8,128)} %beta.1, bf16[32,512,128]{2,1,0:T(8,128)(2,1)} %bitcast.16, bf16[4,32,4096]{2,1,0:T(8,128)(2,1)} %broadcast_select_fusion.em), custom_call_target="tpu_custom_call" | custom-call | flops 1700000000 | bytes 10000000 | tf_op jit(solution)/shard_map/pallas_call | solution.py:405
  315.1 1.4 slice_reduce_fusion
  316.5 2.3 copy.24
  318.8 0.8 copy.25
  319.6 0.8 copy.26
  (29 shorter events, 0.3 us)
Async XLA Ops:
  5.5 4.1 %copy-start.2 = (s32[1408]{0:T(1024)}, s32[1408]{0:T(1024)S(1)}, u32[]{:S(2)}) copy-start(s32[1408]{0:T(1024)S(1)} %constant_dynamic-update-slice_fusion.tab) | copy-start | bytes 16900
  315.0 3.8 %copy-start.1 = (f32[32,4096]{1,0:T(8,128)S(1)}, f32[32,4096]{1,0:T(8,128)}, u32[]{:S(2)}) copy-start(f32[32,4096]{1,0:T(8,128)} %get-tuple-element.27) | copy-start | bytes 1572868
  315.0 4.5 %copy-start = (f32[32,4096]{1,0:T(8,128)S(1)}, f32[32,4096]{1,0:T(8,128)}, u32[]{:S(2)}) copy-start(f32[32,4096]{1,0:T(8,128)} %get-tuple-element.28) | copy-start | bytes 1572868

commit v3 on v2

v3 whole, which is shorter than its diff:
```python
import functools

import jax
import jax.numpy as jnp
from jax import lax
from jax.experimental import pallas as pl
from jax.experimental.pallas import tpu as pltpu
from jax.sharding import PartitionSpec as P

K = 4
STEPS = 4
NZ = 8
NY = 4
NX = 4
CAP = 8
NB = 32
NS = 32
BS = 128
REFS = NB * K
COL = NZ * CAP
CHUNK = 8
PIECES = 4
PIECE = NB // PIECES
TURNS = (4, 3, 5, 2, 6, 1, 7, 0)
EARLY = 5
MESH = pl.DeviceIdType.MESH
F32 = jnp.float32
BF16 = jnp.bfloat16

SEL, REF, INV, ORD, LO, HI = 0, 256, 384, 640, 896, 1152


def index_tables(sources):
    rank = lax.axis_index("state")
    z, y = rank // NY, rank % NY
    rows = lax.dynamic_slice_in_dim(sources.reshape(NZ, NY * REFS), z, 1, 0).reshape(NY, REFS)
    rows = jnp.roll(rows, -y, axis=0)
    owner, local = rows // NB, rows % NB
    ordinal = jnp.arange(REFS, dtype=jnp.int32)
    earlier = (owner[:, None, :] == owner[:, :, None]) & (ordinal[None, :] < ordinal[:, None])[None]
    slot = jnp.sum(earlier.astype(jnp.int32), axis=2)
    ahead = (owner // NY - z) % NZ
    column = owner % NY
    place = ahead * CAP + slot
    spots = jnp.arange(COL, dtype=jnp.int32)
    mine = (column == y)[:, :, None] & (place[:, :, None] == spots)
    sel = jnp.sum(jnp.where(mine, local[:, :, None], 0), axis=1)
    filled = jnp.any(mine, axis=1)
    ref = ((y - column[0]) % NY) * COL + place[0]
    turn = jnp.where(ahead[0] <= 4, jnp.maximum(7 - 2 * ahead[0], 0), 2 * ahead[0] - 8)
    towards = ((column[0] - y) % NY) * COL + turn * CAP + slot[0]
    inv = jnp.sum(
        jnp.where(towards[:, None] == jnp.arange(NY * COL, dtype=jnp.int32), ordinal[:, None], 0), axis=0
    )
    key = jnp.where(filled, sel, NB)
    key = jnp.concatenate([key[:1], key[:0:-1]], axis=0).reshape(NY, NZ, CAP)
    key = key.transpose(1, 0, 2).reshape(NZ, NY * CAP)
    key = jnp.stack([key[d] for d in TURNS])
    number = jnp.arange(NY * CAP, dtype=jnp.int32)
    less = (key[:, None, :] < key[:, :, None]) | (
        (key[:, None, :] == key[:, :, None]) & (number[None, :] < number[:, None])[None]
    )
    rank_of = jnp.sum(less.astype(jnp.int32), axis=2)
    order = jnp.sum(jnp.where(rank_of[:, :, None] == number, number[None, :, None], 0), axis=1)
    blocks = jnp.arange(NB, dtype=jnp.int32)
    low = jnp.sum((key[:, None, :] < blocks[None, :, None]).astype(jnp.int32), axis=2)
    high = jnp.sum((key[:, None, :] <= blocks[None, :, None]).astype(jnp.int32), axis=2)
    return jnp.concatenate([part.reshape(-1).astype(jnp.int32) for part in (sel, ref, inv, order, low, high)])


def loop(count, fn, init=0, width=1):
    def several(i, carry):
        return fn([i * width + n for n in range(width)], carry)

    several.__name__ = fn.__name__
    return lax.fori_loop(0, count // width, several, init)


def body(
    tab, alpha, beta, tr, em,
    counts, alpha_end, beta_start, loglik,
    zg0, zg1, yr0, yr1, yr2, yr3, ys, pb, bsend, br0, br1, bs0, bs1, pre, psv,
    rs_snd, rs_rcv, rl_rcv, w, bacc, cs, cp, cx, cr, sa, sb, sc, sd, scale,
    ag_s, ag_r, bw_s, bw_r, fw_s, fw_r, rs_s, rs_r, sy_s, sy_r, sz_s, sz_r, cp_s, cp_r, ct_s, ct_r,
):
    q, p = lax.axis_index("seq"), lax.axis_index("state")
    z, y = p // NY, p % NY
    x, core = q // 2, q % 2
    zgs, yrs, brs = (zg0, zg1), (yr0, yr1, yr2, yr3), ((br0, bs0), (br1, bs1))
    total_states = float(NB * BS * NZ * NY)

    def at_z(dz):
        return (q, lax.rem(z + dz + NZ, NZ) * NY + y)

    def at_y(dy):
        return (q, z * NY + lax.rem(y + dy, NY))

    def at_x(dx):
        return (lax.rem(x + dx, NX) * 2 + core, p)

    partner = (x * 2 + 1 - core, p)

    barrier = pltpu.get_barrier_semaphore()
    for dz in range(1, NZ):
        pl.semaphore_signal(barrier, inc=1, device_id=at_z(dz), device_id_type=MESH)
    for dy in range(1, NY):
        pl.semaphore_signal(barrier, inc=1, device_id=at_y(dy), device_id_type=MESH)
    for dx in range(1, NX):
        pl.semaphore_signal(barrier, inc=1, device_id=at_x(dx), device_id_type=MESH)
    pl.semaphore_signal(barrier, inc=1, device_id=partner, device_id_type=MESH)

    def remote(src, dst, send, recv, device):
        return pltpu.make_async_remote_copy(
            src_ref=src, dst_ref=dst, send_sem=send, recv_sem=recv, device_id=device, device_id_type=MESH
        )

    def cols(j):
        return pl.ds(pl.multiple_of(j * BS, BS), BS)

    def part(c):
        return pl.ds(c * PIECE, PIECE)

    def travels(way, c):
        return c // (PIECES // 2) == way

    def gather_copy(r, way, h, c):
        zg = zgs[r % 2]
        near, far = (h - 1, h) if way else ((1 - h) % NZ, (-h) % NZ)
        return remote(
            zg.at[near, part(c)], zg.at[far, part(c)],
            ag_s.at[r, way, h - 1, c], ag_r.at[r, way, h - 1, c], at_z(-1 if way else 1),
        )

    def reduce_copy(r, way, h, c):
        if r == 3 and h >= 3:
            d = (h - 5 if way else 5 - h) % NZ
            src, dst = psv.at[d, part(c)], rl_rcv.at[way, h - 3, part(c)]
        else:
            src = rs_snd.at[part(c)] if h == 1 else rs_rcv.at[way, h - 2, part(c)]
            dst = rs_rcv.at[way, h - 1, part(c)]
        return remote(src, dst, rs_s.at[r, way, h - 1, c], rs_r.at[r, way, h - 1, c], at_z(-1 if way else 1))

    def back_copy(r, dy, late):
        src = bsend.at[dy - 1, pl.ds(EARLY, NZ - EARLY) if late else pl.ds(0, EARLY)]
        dst = brs[r % 2][late].at[:, pl.ds(dy * CAP, CAP)]
        return remote(src, dst, bw_s.at[r, late, dy - 1], bw_r.at[r, late, dy - 1], at_y(dy))

    def fetch_copy(r, dy):
        return remote(
            ys.at[dy - 1], yrs[r].at[pl.ds(dy * COL, COL)], fw_s.at[r, dy - 1], fw_r.at[r, dy - 1], at_y(dy)
        )

    def sum_y_copy(n, dy):
        return remote(sa.at[n], sb.at[n, dy - 1], sy_s.at[n, dy - 1], sy_r.at[n, dy - 1], at_y(dy))

    def sum_z_copy(n, dz):
        return remote(sc.at[n], sd.at[n, dz - 1], sz_s.at[n, dz - 1], sz_r.at[n, dz - 1], at_z(dz))

    def core_copy(c):
        piece = pl.ds(c * CHUNK, CHUNK)
        return remote(cs.at[1 - core, :, piece], cp.at[:, piece], cp_s.at[c], cp_r.at[c], partner)

    def counts_copy(c, dx):
        piece = pl.ds(c * CHUNK, CHUNK)
        return remote(
            cx.at[lax.rem(x + dx, NX), piece], cr.at[dx - 1, piece], ct_s.at[c, dx - 1], ct_r.at[c, dx - 1], at_x(dx)
        )

    def sum_over_y(n):
        for dy in range(1, NY):
            sum_y_copy(n, dy).start()

    def sum_over_z(n):
        for dy in range(1, NY):
            sum_y_copy(n, dy).wait()
        sc[n] = sa[n] + sb[n, 0] + sb[n, 1] + sb[n, 2]
        for dz in range(1, NZ):
            sum_z_copy(n, dz).start()

    def sum_result(n):
        for dz in range(1, NZ):
            sum_z_copy(n, dz).wait()
        total = sc[n]
        for dz in range(1, NZ):
            total = total + sd[n, dz - 1]
        return jnp.sum(total, axis=2, keepdims=True) / total_states

    def weigh(r):
        u = STEPS - 1 - r

        def weigh_block(blocks, carry):
            for b in blocks:
                message = beta[:, cols(b)] if r == 0 else bacc[b]
                if r == 3:
                    message = message * scale[1]
                w[u, b] = (em[u, :, cols(b)].astype(F32) * message).astype(BF16)
            return carry

        loop(NB, weigh_block, 0, 4)

    def partials(r):
        u = STEPS - 1 - r

        def partial_block(js, acc):
            outs = [
                lax.dot_general(w[u, j], tr[j], (((1,), (1,)), ((), ())), preferred_element_type=F32) for j in js
            ]
            for j, out in zip(js, outs):
                for k in range(K):
                    piece = out[:, k * BS : (k + 1) * BS]
                    pb[j * K + k] = piece.astype(BF16)
                    if r >= 2:
                        acc = acc + piece
            return acc

        acc = loop(NB, partial_block, jnp.zeros((NS, BS), F32), 4)
        if r >= 2:
            sa[r - 2, 1] = acc

    def send_back(r):
        for late in range(2):
            first, past = (EARLY, NZ) if late else (0, EARLY)
            for dy in (1, 3, 2):

                def pack(turns, carry, dy=dy):
                    for n in turns:
                        base = INV + dy * COL + n * CAP
                        values = [pb[tab[base + c]] for c in range(CAP)]
                        for c in range(CAP):
                            bsend[dy - 1, n, c] = values[c]
                    return carry

                lax.fori_loop(first, past, lambda n, carry, pack=pack: pack([n], carry), 0)
                back_copy(r, dy, late).start()

            def keep(turns, carry, late=late, first=first):
                for n in turns:
                    base = INV + n * CAP
                    values = [pb[tab[base + c]] for c in range(CAP)]
                    for c in range(CAP):
                        brs[r % 2][late][n - first, c] = values[c]
                return carry

            lax.fori_loop(first, past, lambda n, carry, keep=keep: keep([n], carry), 0)

    def relay(r, d):
        turn = TURNS.index(d % NZ)
        late = int(turn >= EARLY)
        br, place = brs[r % 2][late], turn - EARLY * late
        base = turn * NB
        pre[0] = jnp.zeros((NS, BS), F32)

        def add(numbers, acc):
            terms = [br[place, tab[ORD + base + i]] for i in numbers]
            for i, term in zip(numbers, terms):
                acc = acc + term.astype(F32)
                pre[i + 1] = acc
            return acc

        loop(NB, add, jnp.zeros((NS, BS), F32), 8)

        def differ(blocks, carry):
            values = [pre[tab[HI + base + b]] - pre[tab[LO + base + b]] for b in blocks]
            for b, value in zip(blocks, values):
                psv[d % NZ, b] = value
            return carry

        loop(NB, differ, 0, 4)

    def mix(r, c, acc):
        yr = yrs[r]

        def mix_block(numbers, acc):
            js = [c * PIECE + i for i in numbers]
            fetched = [jnp.concatenate([yr[tab[REF + j * K + k]] for k in range(K)], axis=1) for j in js]
            outs = [jnp.dot(f, tr[j], preferred_element_type=F32) for f, j in zip(fetched, js)]
            for j, out in zip(js, outs):
                value = out * em[r, :, cols(j)].astype(F32)
                if r == 3:
                    alpha_end[:, cols(j)] = value
                    acc = acc + value
                else:
                    zgs[(r + 1) % 2][0, j] = value.astype(BF16)
                    if r == 1:
                        acc = acc + value * bacc[j]
            return acc

        return loop(PIECE, mix_block, acc, 4)

    for c in range(PIECES):

        def begin(i, carry, c=c):
            b = c * PIECE + i
            zg0[0, b] = alpha[:, cols(b)].astype(BF16)
            return carry

        lax.fori_loop(0, PIECE, begin, 0)
        if c == 0:
            pl.semaphore_wait(barrier, NZ - 1 + NY - 1 + NX)
        for way in range(2):
            gather_copy(0, way, 1, c).start()
    weigh(0)
    partials(0)
    send_back(0)

    for r in range(STEPS):
        zg, yr = zgs[r % 2], yrs[r]
        for h in range(2, 5):
            for c in range(PIECES):
                for way in range(2):
                    gather_copy(r, way, h - 1, c).wait_recv()
                    if h < 4 or travels(way, c):
                        gather_copy(r, way, h, c).start()
        for c in range(PIECES):
            gather_copy(r, 0 if travels(0, c) else 1, 4, c).wait_recv()

        for dy in range(1, NY):
            back_copy(r, dy, 0).wait()
        relay(r, 4)

        def far(blocks, carry):
            for b in blocks:
                rs_snd[b] = psv[4, b].astype(BF16)
            return carry

        loop(NB, far, 0, 4)
        for c in range(PIECES):
            reduce_copy(r, 0 if travels(0, c) else 1, 1, c).start()
        for dy in (1, 3, 2):

            def choose(ds, carry, dy=dy):
                for d in ds:
                    base = SEL + dy * COL + d * CAP
                    values = [zg[d, tab[base + c]] for c in range(CAP)]
                    for c in range(CAP):
                        ys[dy - 1, d * CAP + c] = values[c]
                return carry

            loop(NZ, choose, 0, 1)
            fetch_copy(r, dy).start()

        def hold(ds, carry):
            for d in ds:
                base = SEL + d * CAP
                values = [zg[d, tab[base + c]] for c in range(CAP)]
                for c in range(CAP):
                    yr[d * CAP + c] = values[c]
            return carry

        loop(NZ, hold, 0, 1)
        if r == 2:
            sum_over_z(0)
        for h in range(2, 5):
            if h == 4:
                for dy in range(1, NY):
                    back_copy(r, dy, 1).wait()
            for way in range(2):
                relay(r, h - 5 if way else 5 - h)
            for c in range(PIECES):
                for way in range(2):
                    d = (h - 5 if way else 5 - h) % NZ
                    received = h > 2 or travels(way, c)
                    if received:
                        reduce_copy(r, way, h - 1, c).wait_recv()

                    def join(numbers, carry, way=way, d=d, h=h, c=c, received=received):
                        for b in [c * PIECE + i for i in numbers]:
                            value = psv[d, b]
                            if r == 3 and h == 4:
                                psv[d, b] = value + rl_rcv[way, 0, b]
                                continue
                            if received:
                                value = value + rs_rcv[way, h - 2, b].astype(F32)
                            if r == 3 and h == 3:
                                psv[d, b] = value
                            else:
                                rs_rcv[way, h - 2, b] = value.astype(BF16)
                        return carry

                    loop(PIECE, join, 0, 4)
                    reduce_copy(r, way, h, c).start()
        relay(r, 0)
        for way in range(2):
            for h in range(1, 5):
                for c in range(PIECES):
                    if h < 4 or travels(way, c):
                        gather_copy(r, way, h, c).wait_send()
        if r < 3:
            for c in range(PIECES):
                for way in range(2):
                    reduce_copy(r, way, 4, c).wait_recv()

                def finish(numbers, carry, c=c):
                    for b in [c * PIECE + i for i in numbers]:
                        bacc[b] = psv[0, b] + rs_rcv[0, 3, b].astype(F32) + rs_rcv[1, 3, b].astype(F32)
                    return carry

                loop(PIECE, finish, 0, 4)
            for way in range(2):
                for h in range(1, 5):
                    for c in range(PIECES):
                        if h > 1 or travels(way, c):
                            reduce_copy(r, way, h, c).wait_send()
            if r == 2:
                means = sum_result(0)
                scale[0] = jnp.broadcast_to(1.0 / means[0], (NS, BS))
                scale[1] = jnp.broadcast_to(1.0 / means[1], (NS, BS))
                scale[2] = jnp.broadcast_to(means[1] / means[0], (NS, BS))
            weigh(r + 1)
            partials(r + 1)
        for dy in range(1, NY):
            fetch_copy(r, dy).wait()
        if r < 3:
            send_back(r + 1)

        if r < 3:
            acc = jnp.zeros((NS, BS), F32)
            for c in range(PIECES):
                acc = mix(r, c, acc)
                for way in range(2):
                    gather_copy(r + 1, way, 1, c).start()
        if r == 1:
            sa[0, 0] = acc
            sum_over_y(0)

    def merge(c):
        core_copy(c).wait()

        def merge_block(i, carry):
            j = c * CHUNK + i
            for xp in range(NX):
                cx[xp, j] = (cs[core, xp, j] + cp[xp, j]).astype(BF16)
            return carry

        lax.fori_loop(0, CHUNK, merge_block, 0)
        for dx in range(1, NX):
            counts_copy(c, dx).start()

    for c in range(NB // CHUNK):

        def tally(i, carry, c=c):
            j = c * CHUNK + i
            left = jnp.concatenate(
                [jnp.concatenate([v[tab[REF + j * K + k]] for k in range(K)], axis=1) for v in yrs], axis=0
            )
            right = jnp.concatenate(
                [(w[t, j].astype(F32) * scale[2 if t == 0 else 0]).astype(BF16) for t in range(STEPS)], axis=0
            )
            out = lax.dot_general(left, right, (((0,), (0,)), ((), ())), preferred_element_type=F32)
            for k in range(K):
                for n in range(8):
                    first = k * BS + n * 16
                    cs[n % 2, n // 2, j, k] = out[first : first + 16]
            return carry

        lax.fori_loop(0, CHUNK, tally, 0)
        core_copy(c).start()
        if c > 0:
            merge(c - 1)
    merge(NB // CHUNK - 1)

    acc = jnp.zeros((NS, BS), F32)
    for c in range(PIECES):
        acc = mix(3, c, acc)
    sa[1, 0] = acc
    sum_over_y(1)
    sum_over_z(1)
    means = sum_result(1)
    start_scale = jnp.broadcast_to(1.0 / means[1], (NS, BS))
    end_scale = jnp.broadcast_to(1.0 / means[0], (NS, BS))
    loglik[...] = jnp.broadcast_to(jnp.log(means[0]), (NS, BS))
    for c in range(PIECES):
        for way in range(2):
            reduce_copy(3, way, 4, c).wait_recv()

        def last(i, carry, c=c):
            b = c * PIECE + i
            beta_start[:, cols(b)] = (psv[0, b] + rl_rcv[0, 1, b] + rl_rcv[1, 1, b]) * start_scale
            alpha_end[:, cols(b)] = alpha_end[:, cols(b)] * end_scale
            return carry

        lax.fori_loop(0, PIECE, last, 0)
    for way in range(2):
        for h in range(1, 5):
            for c in range(PIECES):
                if h > 1 or travels(way, c):
                    reduce_copy(3, way, h, c).wait_send()

    for c in range(NB // CHUNK):
        for dx in range(1, NX):
            counts_copy(c, dx).wait()

        def total(i, carry, c=c):
            j = c * CHUNK + i
            value = cs[core, x, j] + cp[x, j]
            for dx in range(1, NX):
                value = value + cr[dx - 1, j].astype(F32)
            for k in range(K):
                rows = pl.ds(pl.multiple_of(k * BS + q * 16, 16), 16)
                counts[j, k] = value[k] * tr[j, rows, :].astype(F32)
            return carry

        lax.fori_loop(0, CHUNK, total, 0)


def shards(alpha_in, beta_in, transitions, emission_cols, token_ids, sources):
    tables = index_tables(sources)
    em = jnp.take(emission_cols, token_ids.T, axis=0)
    shard = (NB, NS, BS)
    vmem = pl.BlockSpec(memory_space=pltpu.VMEM)
    dma = pltpu.SemaphoreType.DMA
    out = pl.pallas_call(
        body,
        out_shape=(
            jax.ShapeDtypeStruct((NB, K, BS // 8, BS), F32),
            jax.ShapeDtypeStruct((NS, NB * BS), F32),
            jax.ShapeDtypeStruct((NS, NB * BS), F32),
            jax.ShapeDtypeStruct((NS, BS), F32),
        ),
        in_specs=[pl.BlockSpec(memory_space=pltpu.SMEM)] + [vmem] * 4,
        out_specs=(vmem,) * 4,
        scratch_shapes=[
            pltpu.VMEM((NZ,) + shard, BF16),
            pltpu.VMEM((NZ,) + shard, BF16),
            *[pltpu.VMEM((NY * COL, NS, BS), BF16)] * STEPS,
            pltpu.VMEM((NY - 1, COL, NS, BS), BF16),
            pltpu.VMEM((REFS, NS, BS), BF16),
            pltpu.VMEM((NY - 1, NZ, CAP, NS, BS), BF16),
            *[pltpu.VMEM((EARLY, NY * CAP, NS, BS), BF16)] * 2,
            *[pltpu.VMEM((NZ - EARLY, NY * CAP, NS, BS), BF16)] * 2,
            pltpu.VMEM((NB + 1, NS, BS), F32),
            pltpu.VMEM((NZ,) + shard, F32),
            pltpu.VMEM(shard, BF16),
            pltpu.VMEM((2, 4) + shard, BF16),
            pltpu.VMEM((2, 2) + shard, F32),
            pltpu.VMEM((STEPS,) + shard, BF16),
            pltpu.VMEM(shard, F32),
            pltpu.VMEM((2, NX, NB, K, BS // 8, BS), F32),
            pltpu.VMEM((NX, NB, K, BS // 8, BS), F32),
            pltpu.VMEM((NX, NB, K, BS // 8, BS), BF16),
            pltpu.VMEM((NX - 1, NB, K, BS // 8, BS), BF16),
            pltpu.VMEM((2, 2, NS, BS), F32),
            pltpu.VMEM((2, NY - 1, 2, NS, BS), F32),
            pltpu.VMEM((2, 2, NS, BS), F32),
            pltpu.VMEM((2, NZ - 1, 2, NS, BS), F32),
            pltpu.VMEM((3, NS, BS), F32),
            *[dma((STEPS, 2, 4, PIECES))] * 2,
            *[dma((STEPS, 2, NY - 1))] * 2,
            *[dma((STEPS, NY - 1))] * 2,
            *[dma((STEPS, 2, 4, PIECES))] * 2,
            *[dma((2, NY - 1))] * 2,
            *[dma((2, NZ - 1))] * 2,
            *[dma((NB // CHUNK,))] * 2,
            *[dma((NB // CHUNK, NX - 1))] * 2,
        ],
        compiler_params=pltpu.CompilerParams(
            collective_id=0, has_side_effects=True, vmem_limit_bytes=62 * 2**20
        ),
        cost_estimate=pl.CostEstimate(flops=1_700_000_000, bytes_accessed=10_000_000, transcendentals=32),
    )(tables, alpha_in, beta_in, transitions.reshape(NB, K * BS, BS), em)
    return out[0], out[1], out[2], out[3][:, 0]


def solution(mesh):
    placed = (
        P("seq", "state"),
        P("seq", "state"),
        P("state", None, None, None),
        P(None, "state"),
        P("seq", None),
        P(),
    )
    return jax.shard_map(
        shards,
        mesh=mesh,
        in_specs=placed,
        out_specs=(P("state", None, "seq", None), P("seq", "state"), P("seq", "state"), P("seq")),
        check_vma=False,
    )
```

time: 321 us -> 257 us (0.80)
  Pallas kernels: 304 us -> 240 us
    pallas_call x1, Pallas kernels: 304 us -> 240 us  [shards(): pl.pallas_call(body, out_shape=(jax.ShapeDtypeStruct((NB, K, BS // 8, BS)...]
where the time goes in v3:
time: 257 us; the launch traced here: 256 us
  Pallas kernels  240 us (93%)
  local copies, waits for them, and re-layouts  11.9 us (5%)
  other arithmetic  3.93 us (2%)
    pallas_call x1, Pallas kernels, shards(): pl.pallas_call(body, out_shape=(jax.ShapeDtypeStruct((NB, K, BS // 8, BS)...  240 us

profile of v3, /device:TPU:1, one launch (start us, length us, event | category | flops | bytes accessed | tf_op | source)
XLA Modules:
  0.0 256.4 jit_solution(5749282861825201326)
XLA Ops:
  0.7 0.7 compare_and_fusion
  1.4 0.7 compare_select_fusion
  2.1 0.1 reshape.142
  2.2 0.9 copy.11
  3.1 0.3 reshape.130
  3.5 0.2 convert_reduce_fusion
  3.7 0.1 fusion.1
  3.9 0.2 select_reduce_fusion.2
  4.0 0.1 reshape.132
  4.2 0.1 select_reduce_fusion.1
  4.5 0.1 slice.93
  4.6 0.1 slice.91
  4.7 0.1 slice.89
  4.7 0.1 slice.87
  4.9 0.1 slice.83
  5.2 0.5 convert_reduce_fusion.1
  5.9 0.1 select_reduce_fusion
  6.1 4.1 %gather_fusion = bf16[128,4096]{1,0:T(8,128)(2,1)S(1)} fusion(bf16[256,4096]{1,0:T(8,128)(2,1)} %param.9, s32[1024]{0:T(1024)S(1)} %pad_clamp_fusion), kind=kCustom, calls=%fused_computation | custom fusion | bytes 2097664 | tf_op jit(solution)/shard_map/jit(_take)/gather | solution.py:508
  10.2 1.1 broadcast_select_fusion.em
  11.3 239.7 %shard_map.93 = (f32[32,4,16,128]{3,2,1,0:T(8,128)}, f32[32,4096]{1,0:T(8,128)}, f32[32,4096]{1,0:T(8,128)}, f32[32,128]{1,0:T(8,128)}) custom-call(s32[1408]{0:T(1024)} %copy-done.2, f32[32,4096]{1,0:T(8,128)} %alpha.1, f32[32,4096]{1,0:T(8,128)} %beta.1, bf16[32,512,128]{2,1,0:T(8,128)(2,1)} %bitcast.19, bf16[4,32,4096]{2,1,0:T(8,128)(2,1)} %broadcast_select_fusion.em), custom_call_target="tpu_custom_call" | custom-call | flops 1700000000 | bytes 10000000 | tf_op jit(solution)/shard_map/pallas_call | solution.py:512
  251.1 1.4 slice_reduce_fusion
  252.5 2.3 copy.21
  254.8 0.8 copy.22
  255.6 0.8 copy.23
  (34 shorter events, 0.9 us)
Async XLA Ops:
  6.1 4.1 %copy-start.2 = (s32[1408]{0:T(1024)}, s32[1408]{0:T(1024)S(1)}, u32[]{:S(2)}) copy-start(s32[1408]{0:T(1024)S(1)} %constant_dynamic-update-slice_fusion.tab) | copy-start | bytes 16900
  251.1 3.8 %copy-start.1 = (f32[32,4096]{1,0:T(8,128)S(1)}, f32[32,4096]{1,0:T(8,128)}, u32[]{:S(2)}) copy-start(f32[32,4096]{1,0:T(8,128)} %get-tuple-element.36) | copy-start | bytes 1572868
  251.1 4.5 %copy-start = (f32[32,4096]{1,0:T(8,128)S(1)}, f32[32,4096]{1,0:T(8,128)}, u32[]{:S(2)}) copy-start(f32[32,4096]{1,0:T(8,128)} %get-tuple-element.37) | copy-start | bytes 1572868

commit v4 on v3

v4 whole, which is shorter than its diff:
```python
import functools

import jax
import jax.numpy as jnp
from jax import lax
from jax.experimental import pallas as pl
from jax.experimental.pallas import tpu as pltpu
from jax.sharding import PartitionSpec as P

K = 4
STEPS = 4
NZ = 8
NY = 4
NX = 4
CAP = 8
NB = 32
NS = 32
BS = 128
REFS = NB * K
COL = NZ * CAP
CHUNK = 8
PIECES = 4
PIECE = NB // PIECES
TURNS = (4, 3, 5, 2, 6, 1, 7, 0)
LOTS = (0, 3, 5, 7, 8)
NEAR = (0, 1, 7, 2, 6, 3, 5, 4)
GROUPS = (0, 1, 3, 5, 7, 8)
TOKENS = 256
MESH = pl.DeviceIdType.MESH
F32 = jnp.float32
BF16 = jnp.bfloat16

SEL, REF, INV, ORD, LO, HI = 0, 256, 384, 640, 896, 1152


def index_tables(sources):
    rank = lax.axis_index("state")
    z, y = rank // NY, rank % NY
    rows = lax.dynamic_slice_in_dim(sources.reshape(NZ, NY * REFS), z, 1, 0).reshape(NY, REFS)
    rows = jnp.roll(rows, -y, axis=0)
    owner, local = rows // NB, rows % NB
    ordinal = jnp.arange(REFS, dtype=jnp.int32)
    earlier = (owner[:, None, :] == owner[:, :, None]) & (ordinal[None, :] < ordinal[:, None])[None]
    slot = jnp.sum(earlier.astype(jnp.int32), axis=2)
    ahead = (owner // NY - z) % NZ
    column = owner % NY
    place = ahead * CAP + slot
    spots = jnp.arange(COL, dtype=jnp.int32)
    mine = (column == y)[:, :, None] & (place[:, :, None] == spots)
    sel = jnp.sum(jnp.where(mine, local[:, :, None], 0), axis=1)
    filled = jnp.any(mine, axis=1)
    near = jnp.where(ahead[0] <= 3, jnp.maximum(2 * ahead[0] - 1, 0), jnp.minimum(16 - 2 * ahead[0], 7))
    ref = ((y - column[0]) % NY) * COL + near * CAP + slot[0]
    turn = jnp.where(ahead[0] <= 4, jnp.maximum(7 - 2 * ahead[0], 0), 2 * ahead[0] - 8)
    towards = ((column[0] - y) % NY) * COL + turn * CAP + slot[0]
    inv = jnp.sum(
        jnp.where(towards[:, None] == jnp.arange(NY * COL, dtype=jnp.int32), ordinal[:, None], 0), axis=0
    )
    key = jnp.where(filled, sel, NB)
    key = jnp.concatenate([key[:1], key[:0:-1]], axis=0).reshape(NY, NZ, CAP)
    key = key.transpose(1, 0, 2).reshape(NZ, NY * CAP)
    key = jnp.stack([key[d] for d in TURNS])
    number = jnp.arange(NY * CAP, dtype=jnp.int32)
    less = (key[:, None, :] < key[:, :, None]) | (
        (key[:, None, :] == key[:, :, None]) & (number[None, :] < number[:, None])[None]
    )
    rank_of = jnp.sum(less.astype(jnp.int32), axis=2)
    order = jnp.sum(jnp.where(rank_of[:, :, None] == number, number[None, :, None], 0), axis=1)
    blocks = jnp.arange(NB, dtype=jnp.int32)
    low = jnp.sum((key[:, None, :] < blocks[None, :, None]).astype(jnp.int32), axis=2)
    high = jnp.sum((key[:, None, :] <= blocks[None, :, None]).astype(jnp.int32), axis=2)
    return jnp.concatenate([part.reshape(-1).astype(jnp.int32) for part in (sel, ref, inv, order, low, high)])


def loop(count, fn, init=0, width=1):
    def several(i, carry):
        return fn([i * width + n for n in range(width)], carry)

    several.__name__ = fn.__name__
    return lax.fori_loop(0, count // width, several, init)


def body(
    tab, hot, alpha_hbm, beta_hbm, tr_hbm, cols_hbm,
    counts, alpha_end, beta_start, loglik,
    za0, za1, za2, za3, za4, za5, za6, za7, zb0, zb1, zb2, zb3, zb4, zb5, zb6, zb7,
    em, yr0, yr1, yr2, yr3, ys, pb, bsend, ba0, ba1, ba2, ba3, bb0, bb1, bb2, bb3, pre, psv,
    rs_snd, rs_rcv, rl_rcv, w, bacc, cs, cp, cx, cr, sa, sp, sb, sc, sd, scale, alpha, beta, tr, cols_in, ld,
    ag_s, ag_r, bw_s, bw_r, fw_s, fw_r, rs_s, rs_r, sy_s, sy_r, sz_s, sz_r, cp_s, cp_r, ct_s, ct_r,
):
    q, p = lax.axis_index("seq"), lax.axis_index("state")
    z, y = p // NY, p % NY
    x, core = q // 2, q % 2
    zgs = (za0, za1, za2, za3, za4, za5, za6, za7), (zb0, zb1, zb2, zb3, zb4, zb5, zb6, zb7)
    yrs, brs = (yr0, yr1, yr2, yr3), ((ba0, ba1, ba2, ba3), (bb0, bb1, bb2, bb3))
    total_states = float(NB * BS * NZ * NY)

    def at_z(dz):
        return (q, lax.rem(z + dz + NZ, NZ) * NY + y)

    def at_y(dy):
        return (q, z * NY + lax.rem(y + dy, NY))

    def at_x(dx):
        return (lax.rem(x + dx, NX) * 2 + core, p)

    partner = (x * 2 + 1 - core, p)

    loads = [
        pltpu.make_async_copy(src, dst, ld.at[n])
        for n, (src, dst) in enumerate(((alpha_hbm, alpha), (cols_hbm, cols_in), (beta_hbm, beta), (tr_hbm, tr)))
    ]
    for load in loads:
        load.start()
    barrier = pltpu.get_barrier_semaphore()
    for dz in range(1, NZ):
        pl.semaphore_signal(barrier, inc=1, device_id=at_z(dz), device_id_type=MESH)
    for dy in range(1, NY):
        pl.semaphore_signal(barrier, inc=1, device_id=at_y(dy), device_id_type=MESH)
    for dx in range(1, NX):
        pl.semaphore_signal(barrier, inc=1, device_id=at_x(dx), device_id_type=MESH)
    pl.semaphore_signal(barrier, inc=1, device_id=partner, device_id_type=MESH)

    def remote(src, dst, send, recv, device):
        return pltpu.make_async_remote_copy(
            src_ref=src, dst_ref=dst, send_sem=send, recv_sem=recv, device_id=device, device_id_type=MESH
        )

    def cols(j):
        return pl.ds(pl.multiple_of(j * BS, BS), BS)

    def part(c):
        return pl.ds(c * PIECE, PIECE)

    def travels(way, c):
        return c // (PIECES // 2) == way

    def gather_copy(r, way, h, c):
        zg = zgs[r % 2]
        near, far = (h - 1, h) if way else ((1 - h) % NZ, (-h) % NZ)
        return remote(
            zg[near].at[part(c)], zg[far].at[part(c)],
            ag_s.at[r, way, h - 1, c], ag_r.at[r, way, h - 1, c], at_z(-1 if way else 1),
        )

    def reduce_copy(r, way, h, c):
        if r == 3 and h >= 3:
            d = (h - 5 if way else 5 - h) % NZ
            src, dst = psv.at[d, part(c)], rl_rcv.at[way, h - 3, part(c)]
        else:
            src = rs_snd.at[part(c)] if h == 1 else rs_rcv.at[r % 2, way, h - 2, part(c)]
            dst = rs_rcv.at[r % 2, way, h - 1, part(c)]
        return remote(src, dst, rs_s.at[r, way, h - 1, c], rs_r.at[r, way, h - 1, c], at_z(-1 if way else 1))

    def back_copy(r, dy, lot):
        src = bsend.at[dy - 1, pl.ds(LOTS[lot], LOTS[lot + 1] - LOTS[lot])]
        dst = brs[r % 2][lot].at[:, pl.ds(dy * CAP, CAP)]
        return remote(src, dst, bw_s.at[r, lot, dy - 1], bw_r.at[r, lot, dy - 1], at_y(dy))

    def fetch_copy(r, dy, g):
        first, rows = GROUPS[g] * CAP, (GROUPS[g + 1] - GROUPS[g]) * CAP
        return remote(
            ys.at[dy - 1, pl.ds(first, rows)], yrs[r].at[pl.ds(dy * COL + first, rows)],
            fw_s.at[r, g, dy - 1], fw_r.at[r, g, dy - 1], at_y(dy),
        )

    def sum_y_copy(n, dy):
        return remote(sp.at[n], sb.at[n, dy - 1], sy_s.at[n, dy - 1], sy_r.at[n, dy - 1], at_y(dy))

    def sum_z_copy(n, dz):
        return remote(sc.at[n], sd.at[n, dz - 1], sz_s.at[n, dz - 1], sz_r.at[n, dz - 1], at_z(dz))

    def core_copy(c):
        piece = pl.ds(c * CHUNK, CHUNK)
        return remote(cs.at[1 - core, :, piece], cp.at[:, piece], cp_s.at[c], cp_r.at[c], partner)

    def counts_copy(c, dx):
        piece = pl.ds(c * CHUNK, CHUNK)
        return remote(
            cx.at[lax.rem(x + dx, NX), piece], cr.at[dx - 1, piece], ct_s.at[c, dx - 1], ct_r.at[c, dx - 1], at_x(dx)
        )

    def sum_over_y(n):
        sp[n] = jnp.zeros((8, BS), F32)
        for m in range(2):
            sp[n, m : m + 1, :NS] = jnp.sum(sa[n, m].T, axis=0, keepdims=True)
        for dy in range(1, NY):
            sum_y_copy(n, dy).start()

    def sum_over_z(n):
        for dy in range(1, NY):
            sum_y_copy(n, dy).wait()
        sc[n] = sp[n] + sb[n, 0] + sb[n, 1] + sb[n, 2]
        for dz in range(1, NZ):
            sum_z_copy(n, dz).start()

    def sum_result(n):
        for dz in range(1, NZ):
            sum_z_copy(n, dz).wait()
        total = sc[n]
        for dz in range(1, NZ):
            total = total + sd[n, dz - 1]
        total = total / total_states
        return [jnp.broadcast_to(total[m : m + 1, :NS], (BS, NS)).T for m in range(2)]

    def weigh(r):
        u = STEPS - 1 - r

        def weigh_block(blocks, carry):
            for b in blocks:
                message = beta[:, cols(b)] if r == 0 else bacc[b]
                if r == 3:
                    message = message * scale[1]
                w[u, b] = (em[u, :, cols(b)].astype(F32) * message).astype(BF16)
            return carry

        loop(NB, weigh_block, 0, 4)

    def partials(r):
        u = STEPS - 1 - r

        def partial_block(js, acc):
            outs = [
                lax.dot_general(w[u, j], tr[j], (((1,), (1,)), ((), ())), preferred_element_type=F32) for j in js
            ]
            for j, out in zip(js, outs):
                for k in range(K):
                    piece = out[:, k * BS : (k + 1) * BS]
                    pb[j * K + k] = piece.astype(BF16)
                    if r >= 2:
                        acc = acc + piece
            return acc

        acc = loop(NB, partial_block, jnp.zeros((NS, BS), F32), 4)
        if r >= 2:
            sa[r - 2, 1] = acc

    def send_back(r, lot):
        first, past = LOTS[lot], LOTS[lot + 1]
        for dy in (1, 3, 2):

            def pack(turns, carry, dy=dy):
                for n in turns:
                    base = INV + dy * COL + n * CAP
                    values = [pb[tab[base + c]] for c in range(CAP)]
                    for c in range(CAP):
                        bsend[dy - 1, n, c] = values[c]
                return carry

            lax.fori_loop(first, past, lambda n, carry, pack=pack: pack([n], carry), 0)
            back_copy(r, dy, lot).start()

        def keep(turns, carry, lot=lot, first=first):
            for n in turns:
                base = INV + n * CAP
                values = [pb[tab[base + c]] for c in range(CAP)]
                for c in range(CAP):
                    brs[r % 2][lot][n - first, c] = values[c]
            return carry

        lax.fori_loop(first, past, lambda n, carry, keep=keep: keep([n], carry), 0)

    def relay(r, d):
        turn = TURNS.index(d % NZ)
        lot = sum(turn >= first for first in LOTS[1:-1])
        br, place = brs[r % 2][lot], turn - LOTS[lot]
        base = turn * NB
        pre[0] = jnp.zeros((NS, BS), F32)

        def add(numbers, acc):
            terms = [br[place, tab[ORD + base + i]] for i in numbers]
            for i, term in zip(numbers, terms):
                acc = acc + term.astype(F32)
                pre[i + 1] = acc
            return acc

        loop(NB, add, jnp.zeros((NS, BS), F32), 8)

        def differ(blocks, carry):
            values = [pre[tab[HI + base + b]] - pre[tab[LO + base + b]] for b in blocks]
            for b, value in zip(blocks, values):
                psv[d % NZ, b] = value
            return carry

        loop(NB, differ, 0, 4)

    def mix(r, c, acc):
        yr = yrs[r]

        def mix_block(numbers, acc):
            js = [c * PIECE + i for i in numbers]
            fetched = [jnp.concatenate([yr[tab[REF + j * K + k]] for k in range(K)], axis=1) for j in js]
            outs = [jnp.dot(f, tr[j], preferred_element_type=F32) for f, j in zip(fetched, js)]
            for j, out in zip(js, outs):
                value = out * em[r, :, cols(j)].astype(F32)
                if r == 3:
                    alpha_end[:, cols(j)] = value
                    acc = acc + value
                else:
                    zgs[(r + 1) % 2][0][j] = value.astype(BF16)
            return acc

        return loop(PIECE, mix_block, acc, 4)

    def choose(r, g):
        zg, yr = zgs[r % 2], yrs[r]
        for n in range(GROUPS[g], GROUPS[g + 1]):
            d = NEAR[n]
            base = SEL + d * CAP

            def choose_one(dy, carry, n=n, d=d, base=base):
                values = [zg[d][tab[base + dy * COL + c]] for c in range(CAP)]
                for c in range(CAP):
                    ys[dy - 1, n * CAP + c] = values[c]
                return carry

            lax.fori_loop(1, NY, choose_one, 0)
        for dy in (1, 3, 2):
            fetch_copy(r, dy, g).start()
        for n in range(GROUPS[g], GROUPS[g + 1]):
            values = [zg[NEAR[n]][tab[SEL + NEAR[n] * CAP + c]] for c in range(CAP)]
            for c in range(CAP):
                yr[n * CAP + c] = values[c]

    def pass_on(r, h):
        for c in range(PIECES):
            for way in range(2):
                gather_copy(r, way, h - 1, c).wait_recv()
                if h < 4 or travels(way, c):
                    gather_copy(r, way, h, c).start()

    def gather_end(r):
        for c in range(PIECES):
            gather_copy(r, 0 if travels(0, c) else 1, 4, c).wait_recv()

    def reduce_step(r, h):
        if h == 1:
            relay(r, 4)

            def far(blocks, carry):
                for b in blocks:
                    rs_snd[b] = psv[4, b].astype(BF16)
                return carry

            loop(NB, far, 0, 4)
            for c in range(PIECES):
                reduce_copy(r, 0 if travels(0, c) else 1, 1, c).start()
            return
        for way in range(2):
            relay(r, h - 5 if way else 5 - h)
        for c in range(PIECES):
            for way in range(2):
                d = (h - 5 if way else 5 - h) % NZ
                received = h > 2 or travels(way, c)
                if received:
                    reduce_copy(r, way, h - 1, c).wait_recv()

                def join(numbers, carry, way=way, d=d, c=c, received=received):
                    for b in [c * PIECE + i for i in numbers]:
                        value = psv[d, b]
                        if r == 3 and h == 4:
                            psv[d, b] = value + rl_rcv[way, 0, b]
                            continue
                        if received:
                            value = value + rs_rcv[r % 2, way, h - 2, b].astype(F32)
                        if r == 3 and h == 3:
                            psv[d, b] = value
                        else:
                            rs_rcv[r % 2, way, h - 2, b] = value.astype(BF16)
                    return carry

                loop(PIECE, join, 0, 4)
                reduce_copy(r, way, h, c).start()

    def reduce_end(r):
        acc = jnp.zeros((NS, BS), F32)
        for c in range(PIECES):
            for way in range(2):
                reduce_copy(r, way, 4, c).wait_recv()

            def finish(numbers, acc, c=c):
                for b in [c * PIECE + i for i in numbers]:
                    value = psv[0, b] + rs_rcv[r % 2, 0, 3, b].astype(F32) + rs_rcv[r % 2, 1, 3, b].astype(F32)
                    bacc[b] = value
                    if r == 1:
                        acc = acc + value * zgs[0][0][b].astype(F32)
                return acc

            acc = loop(PIECE, finish, acc, 4)
        if r == 1:
            sa[0, 0] = acc
        for way in range(2):
            for h in range(1, 5):
                for c in range(PIECES):
                    if h > 1 or travels(way, c):
                        reduce_copy(r, way, h, c).wait_send()

    loads[0].wait()
    for c in range(PIECES):

        def begin(numbers, carry, c=c):
            for b in [c * PIECE + i for i in numbers]:
                za0[b] = alpha[:, cols(b)].astype(BF16)
            return carry

        loop(PIECE, begin, 0, 4)
        if c == 0:
            pl.semaphore_wait(barrier, NZ - 1 + NY - 1 + NX)
        for way in range(2):
            gather_copy(0, way, 1, c).start()
    choose(0, 0)

    def emit(i, carry):
        span = pl.ds(pl.multiple_of(i * 256, 256), 256)
        rows = jnp.dot(hot[...], cols_in[:, span], preferred_element_type=F32).astype(BF16)
        for t in range(STEPS):
            em[t, :, span] = rows[t * NS : (t + 1) * NS]
        return carry

    loads[1].wait()
    lax.fori_loop(0, NB * BS // 256, emit, 0)
    loads[2].wait()
    weigh(0)
    loads[3].wait()
    partials(0)
    pass_on(0, 2)
    choose(0, 1)
    pass_on(0, 3)
    choose(0, 2)
    pass_on(0, 4)
    choose(0, 3)
    gather_end(0)
    choose(0, 4)

    def await_back(r, lot):
        for dy in range(1, NY):
            back_copy(r, dy, lot).wait()

    for r in range(STEPS):
        for g in range(len(GROUPS) - 1):
            if g == len(GROUPS) - 2:
                send_back(r, 0)
            for dy in range(1, NY):
                fetch_copy(r, dy, g).wait()
        for lot in range(1, len(LOTS) - 1):
            send_back(r, lot)
        for way in range(2):
            for h in range(1, 5):
                for c in range(PIECES):
                    if h < 4 or travels(way, c):
                        gather_copy(r, way, h, c).wait_send()
        if r == 2:
            sum_over_z(0)
        if r < 3:
            acc = jnp.zeros((NS, BS), F32)
            for c in range(PIECES):
                mix(r, c, acc)
                for way in range(2):
                    gather_copy(r + 1, way, 1, c).start()
            for h in range(2, 5):
                pass_on(r + 1, h)
            for g in range(3):
                choose(r + 1, g)
            await_back(r, 0)
            reduce_step(r, 1)
            choose(r + 1, 3)
            gather_end(r + 1)
            choose(r + 1, 4)
            reduce_step(r, 2)
            await_back(r, 1)
            reduce_step(r, 3)
            await_back(r, 2)
            reduce_step(r, 4)
            await_back(r, 3)
            relay(r, 0)
            reduce_end(r)
            if r == 2:
                means = sum_result(0)
                scale[0] = 1.0 / means[0]
                scale[1] = 1.0 / means[1]
                scale[2] = means[1] / means[0]
            weigh(r + 1)
            partials(r + 1)
            if r == 1:
                sum_over_y(0)

    def merge(c):
        core_copy(c).wait()

        def merge_block(i, carry):
            j = c * CHUNK + i
            for xp in range(NX):
                cx[xp, j] = (cs[core, xp, j] + cp[xp, j]).astype(BF16)
            return carry

        lax.fori_loop(0, CHUNK, merge_block, 0)
        for dx in range(1, NX):
            counts_copy(c, dx).start()

    for c in range(NB // CHUNK):

        def tally(i, carry, c=c):
            j = c * CHUNK + i
            left = jnp.concatenate(
                [jnp.concatenate([v[tab[REF + j * K + k]] for k in range(K)], axis=1) for v in yrs], axis=0
            )
            right = jnp.concatenate(
                [(w[t, j].astype(F32) * scale[2 if t == 0 else 0]).astype(BF16) for t in range(STEPS)], axis=0
            )
            out = lax.dot_general(left, right, (((0,), (0,)), ((), ())), preferred_element_type=F32)
            for k in range(K):
                for n in range(8):
                    first = k * BS + n * 16
                    cs[n % 2, n // 2, j, k] = out[first : first + 16]
            return carry

        lax.fori_loop(0, CHUNK, tally, 0)
        core_copy(c).start()

    acc = jnp.zeros((NS, BS), F32)
    for c in range(PIECES):
        acc = mix(3, c, acc)
    sa[1, 0] = acc
    sum_over_y(1)
    await_back(3, 0)
    reduce_step(3, 1)
    sum_over_z(1)
    reduce_step(3, 2)
    for c in range(NB // CHUNK):
        merge(c)
    await_back(3, 1)
    reduce_step(3, 3)
    await_back(3, 2)
    reduce_step(3, 4)
    await_back(3, 3)
    relay(3, 0)

    def total(c):
        for dx in range(1, NX):
            counts_copy(c, dx).wait()

        def total_block(i, carry):
            j = c * CHUNK + i
            value = cs[core, x, j] + cp[x, j]
            for dx in range(1, NX):
                value = value + cr[dx - 1, j].astype(F32)
            for k in range(K):
                rows = pl.ds(pl.multiple_of(k * BS + q * 16, 16), 16)
                counts[j, k] = value[k] * tr[j, rows, :].astype(F32)
            return carry

        lax.fori_loop(0, CHUNK, total_block, 0)

    means = sum_result(1)
    start_scale = 1.0 / means[1]
    end_scale = 1.0 / means[0]
    loglik[...] = jnp.log(means[0])

    def settle(b, carry):
        alpha_end[:, cols(b)] = alpha_end[:, cols(b)] * end_scale
        return carry

    lax.fori_loop(0, NB, settle, 0)
    for c in range(NB // CHUNK):
        total(c)
    for c in range(PIECES):
        for way in range(2):
            reduce_copy(3, way, 4, c).wait_recv()

        def last(i, carry, c=c):
            b = c * PIECE + i
            beta_start[:, cols(b)] = (psv[0, b] + rl_rcv[0, 1, b] + rl_rcv[1, 1, b]) * start_scale
            return carry

        lax.fori_loop(0, PIECE, last, 0)
    for way in range(2):
        for h in range(1, 5):
            for c in range(PIECES):
                if h > 1 or travels(way, c):
                    reduce_copy(3, way, h, c).wait_send()


def shards(alpha_in, beta_in, transitions, emission_cols, token_ids, sources):
    tables = index_tables(sources)
    hot = (token_ids.T.reshape(STEPS * NS, 1) == jnp.arange(TOKENS, dtype=jnp.int32)).astype(BF16)
    shard = (NB, NS, BS)
    vmem = pl.BlockSpec(memory_space=pltpu.VMEM)
    dma = pltpu.SemaphoreType.DMA
    out = pl.pallas_call(
        body,
        out_shape=(
            jax.ShapeDtypeStruct((NB, K, BS // 8, BS), F32),
            jax.ShapeDtypeStruct((NS, NB * BS), F32),
            jax.ShapeDtypeStruct((NS, NB * BS), F32),
            jax.ShapeDtypeStruct((NS, BS), F32),
        ),
        in_specs=[pl.BlockSpec(memory_space=pltpu.SMEM), vmem] + [pl.BlockSpec(memory_space=pl.ANY)] * 4,
        out_specs=(vmem,) * 4,
        scratch_shapes=[
            *[pltpu.VMEM(shard, BF16)] * (2 * NZ),
            pltpu.VMEM((STEPS, NS, NB * BS), BF16),
            *[pltpu.VMEM((NY * COL, NS, BS), BF16)] * STEPS,
            pltpu.VMEM((NY - 1, COL, NS, BS), BF16),
            pltpu.VMEM((REFS, NS, BS), BF16),
            pltpu.VMEM((NY - 1, NZ, CAP, NS, BS), BF16),
            *[pltpu.VMEM((LOTS[n + 1] - LOTS[n], NY * CAP, NS, BS), BF16) for n in (0, 1, 2, 3) * 2],
            pltpu.VMEM((NB + 1, NS, BS), F32),
            pltpu.VMEM((NZ,) + shard, F32),
            pltpu.VMEM(shard, BF16),
            pltpu.VMEM((2, 2, 4) + shard, BF16),
            pltpu.VMEM((2, 2) + shard, F32),
            pltpu.VMEM((STEPS,) + shard, BF16),
            pltpu.VMEM(shard, F32),
            pltpu.VMEM((2, NX, NB, K, BS // 8, BS), F32),
            pltpu.VMEM((NX, NB, K, BS // 8, BS), F32),
            pltpu.VMEM((NX, NB, K, BS // 8, BS), BF16),
            pltpu.VMEM((NX - 1, NB, K, BS // 8, BS), BF16),
            pltpu.VMEM((2, 2, NS, BS), F32),
            pltpu.VMEM((2, 8, BS), F32),
            pltpu.VMEM((2, NY - 1, 8, BS), F32),
            pltpu.VMEM((2, 8, BS), F32),
            pltpu.VMEM((2, NZ - 1, 8, BS), F32),
            pltpu.VMEM((3, NS, BS), F32),
            pltpu.VMEM((NS, NB * BS), F32),
            pltpu.VMEM((NS, NB * BS), F32),
            pltpu.VMEM((NB, K * BS, BS), BF16),
            pltpu.VMEM((TOKENS, NB * BS), BF16),
            dma((4,)),
            *[dma((STEPS, 2, 4, PIECES))] * 2,
            *[dma((STEPS, len(LOTS) - 1, NY - 1))] * 2,
            *[dma((STEPS, len(GROUPS) - 1, NY - 1))] * 2,
            *[dma((STEPS, 2, 4, PIECES))] * 2,
            *[dma((2, NY - 1))] * 2,
            *[dma((2, NZ - 1))] * 2,
            *[dma((NB // CHUNK,))] * 2,
            *[dma((NB // CHUNK, NX - 1))] * 2,
        ],
        compiler_params=pltpu.CompilerParams(
            collective_id=0, has_side_effects=True, vmem_limit_bytes=62 * 2**20
        ),
        cost_estimate=pl.CostEstimate(flops=1_700_000_000, bytes_accessed=10_000_000, transcendentals=32),
    )(tables, hot, alpha_in, beta_in, transitions.reshape(NB, K * BS, BS), emission_cols)
    return out[0], out[1], out[2], out[3][:, 0]


def solution(mesh):
    placed = (
        P("seq", "state"),
        P("seq", "state"),
        P("state", None, None, None),
        P(None, "state"),
        P("seq", None),
        P(),
    )
    return jax.shard_map(
        shards,
        mesh=mesh,
        in_specs=placed,
        out_specs=(P("state", None, "seq", None), P("seq", "state"), P("seq", "state"), P("seq")),
        check_vma=False,
    )
```

time: 257 us -> 248 us (0.965)
  Pallas kernels: 240 us -> 232 us
    pallas_call x1, Pallas kernels: 240 us -> 232 us  [shards(): pl.pallas_call(body, out_shape=(jax.ShapeDtypeStruct((NB, K, BS // 8, BS)...]
    gather x1 -> x0, local copies, waits for them, and re-layouts: 4.07 us -> none  [shards(): em = jnp.take(emission_cols, token_ids.T, axis=0)]
    unnamed x14 -> x10, local copies, waits for them, and re-layouts: 4.87 us -> 7.6 us
where the time goes in v4:
time: 248 us; the launch traced here: 246 us
  Pallas kernels  232 us (94%)
  local copies, waits for them, and re-layouts  11.2 us (5%)
    pallas_call x1, Pallas kernels, shards(): pl.pallas_call(body, out_shape=(jax.ShapeDtypeStruct((NB, K, BS // 8, BS)...  232 us
    unnamed x10, local copies, waits for them, and re-layouts  7.6 us

profile of v4, /device:TPU:1, one launch (start us, length us, event | category | flops | bytes accessed | tf_op | source)
XLA Modules:
  0.0 245.8 jit_solution(8090189780176220947)
XLA Ops:
  0.7 0.8 eq.109
  1.5 0.7 fusion.2.hot
  2.2 0.9 copy.11
  3.1 0.3 reshape.138
  3.5 0.2 convert_reduce_fusion
  3.7 0.1 fusion.1
  3.9 0.2 select_reduce_fusion.2
  4.0 0.1 reshape.140
  4.2 0.1 select_reduce_fusion.1
  4.5 0.1 slice.93
  4.6 0.1 slice.91
  4.7 0.1 slice.89
  4.7 0.1 slice.87
  4.8 0.1 slice.85
  4.9 0.1 slice.83
  5.0 0.1 slice.81
  5.2 0.5 convert_reduce_fusion.1
  5.9 0.1 select_reduce_fusion
  6.1 0.6 copy-done
  6.7 231.7 %shard_map.93 = (f32[32,4,16,128]{3,2,1,0:T(8,128)}, f32[32,4096]{1,0:T(8,128)}, f32[32,4096]{1,0:T(8,128)}, f32[32,128]{1,0:T(8,128)}) custom-call(s32[1408]{0:T(1024)} %copy-done, bf16[128,256]{1,0:T(8,128)(2,1)} %fusion.2.hot, f32[32,4096]{1,0:T(8,128)} %alpha_hbm.1, f32[32,4096]{1,0:T(8,128)} %beta_hbm.1, bf16[32,512,128]{2,1,0:T(8,128)(2,1)} %bitcast.15, ...), custom_call_target="tpu_custom_call" | custom-call | flops 1700000000 | bytes 10000000 | tf_op jit(solution)/shard_map/pallas_call | solution.py:589
  238.5 1.3 slice_reduce_fusion
  239.8 2.3 copy.21
  242.1 1.9 copy.22
  244.0 1.9 copy.23
  (26 shorter events, 0.7 us)
Async XLA Ops:
  6.1 0.6 copy-start

commit v5 on v4

--- a/solution.py
+++ b/solution.py
@@ -19,7 +19,7 @@
 REFS = NB * K
 COL = NZ * CAP
 CHUNK = 8
-PIECES = 4
+PIECES = 8
 PIECE = NB // PIECES
 TURNS = (4, 3, 5, 2, 6, 1, 7, 0)
 LOTS = (0, 3, 5, 7, 8)

time: 248 us -> 253 us (1.020)
  Pallas kernels: 232 us -> 235 us
    pallas_call x1, Pallas kernels: 232 us -> 235 us  [shards(): pl.pallas_call(body, out_shape=(jax.ShapeDtypeStruct((NB, K, BS // 8, BS)...]
where the time goes in v5:
time: 253 us; the launch traced here: 249 us
  Pallas kernels  235 us (93%)
  local copies, waits for them, and re-layouts  11.2 us (4%)
    pallas_call x1, Pallas kernels, shards(): pl.pallas_call(body, out_shape=(jax.ShapeDtypeStruct((NB, K, BS // 8, BS)...  235 us
    unnamed x10, local copies, waits for them, and re-layouts  7.6 us

profile of v5, /device:TPU:1, one launch (start us, length us, event | category | flops | bytes accessed | tf_op | source)
XLA Modules:
  0.0 249.5 jit_solution(404372055895685388)
XLA Ops:
  0.7 0.8 eq.109
  1.5 0.7 fusion.2.hot
  2.2 0.9 copy.11
  3.1 0.3 reshape.138
  3.5 0.2 convert_reduce_fusion
  3.7 0.1 fusion.1
  3.9 0.2 select_reduce_fusion.2
  4.0 0.1 reshape.140
  4.2 0.1 select_reduce_fusion.1
  4.5 0.1 slice.93
  4.6 0.1 slice.91
  4.7 0.1 slice.89
  4.7 0.1 slice.87
  4.8 0.1 slice.85
  4.9 0.1 slice.83
  5.0 0.1 slice.81
  5.2 0.5 convert_reduce_fusion.1
  5.9 0.1 select_reduce_fusion
  6.1 0.6 copy-done
  6.7 235.4 %shard_map.93 = (f32[32,4,16,128]{3,2,1,0:T(8,128)}, f32[32,4096]{1,0:T(8,128)}, f32[32,4096]{1,0:T(8,128)}, f32[32,128]{1,0:T(8,128)}) custom-call(s32[1408]{0:T(1024)} %copy-done, bf16[128,256]{1,0:T(8,128)(2,1)} %fusion.2.hot, f32[32,4096]{1,0:T(8,128)} %alpha_hbm.1, f32[32,4096]{1,0:T(8,128)} %beta_hbm.1, bf16[32,512,128]{2,1,0:T(8,128)(2,1)} %bitcast.15, ...), custom_call_target="tpu_custom_call" | custom-call | flops 1700000000 | bytes 10000000 | tf_op jit(solution)/shard_map/pallas_call | solution.py:589
  242.1 1.3 slice_reduce_fusion
  243.4 2.3 copy.21
  245.7 1.9 copy.22
  247.6 1.9 copy.23
  (26 shorter events, 0.7 us)
Async XLA Ops:
  6.1 0.6 copy-start
